TPU v7x, 512 devices: a whole 4x8x8 slice. The times are simulated.
512 devices in a mesh: gx: 8 (over x, core), gy: 8 (over y), gz: 8 (over z).
Axes of the slice: x: 4, y: 8, z: 8, core: 2. Of those that a mesh axis runs over, the one named last changes fastest.
Arguments:
- loads: float32 [3, 64, 64, 1024], P(None, 'gx', 'gy', 'gz'), may hold values from -6 to 6
- density: float32 [64, 64, 1024], P('gx', 'gy', 'gz'), may hold values from 0.2 to 1
Outputs:
- solution: float32 [3, 64, 64, 1024], P(None, 'gx', 'gy', 'gz')
All inputs are finite; a program needn't handle non-finite values.
Results may differ from a plain program's by a relative error of at most 0.0001.
Values sent between devices are 32-bit elements; how exact they have to be, the bound alone decides.
A program may use at most 64 MiB of HBM per device.

v0:
```python
import jax
import jax.numpy as jnp
from jax import lax
from jax.sharding import PartitionSpec as P

LEVELS = 4
SWEEPS = 2
COARSE = 8


damping = 0.6
floor_modulus = 0.001
offsets = [(bit_x, bit_y, bit_z) for bit_x in (0, 1) for bit_y in (0, 1) for bit_z in (0, 1)]


def extended(cells, sides, width):
    for axis, dim in sides:
        count = lax.axis_size(axis)
        ends = count - 1
        head = lax.slice_in_dim(cells, 0, width, axis=dim)
        tail = lax.slice_in_dim(cells, cells.shape[dim] - width, cells.shape[dim], axis=dim)
        cells = jnp.concatenate(
            [
                lax.ppermute(tail, axis, [(i, (i + 1) % count) for i in range(ends)]),
                cells,
                lax.ppermute(head, axis, [((i + 1) % count, i) for i in range(ends)]),
            ],
            axis=dim,
        )
    return cells


def differs_once(first, second):
    return sum((1 for place in range(3) if first[place] != second[place])) == 1


def take_block(array, start, count):
    return array[
        :,
        start[0] : start[0] + count[0],
        start[1] : start[1] + count[1],
        start[2] : start[2] + count[2],
    ]


def apply_stiffness(padded_field, padded_moduli, scale):
    dims = padded_field.shape[1:]
    count = tuple((size - 1 for size in dims))
    out_count = tuple((size - 2 for size in dims))
    corner_values = {}
    for bits in offsets:
        corner_values[bits] = take_block(padded_field, bits, count)
    total = corner_values[offsets[0]]
    for bits in offsets[1:]:
        total = total + corner_values[bits]
    element = take_block(padded_moduli, (0, 0, 0), count)
    result = None
    for bits in offsets:
        edges = None
        for other in offsets:
            if differs_once(bits, other):
                edges = corner_values[other] if edges is None else edges + corner_values[other]
        contribution = element * (5.0 * corner_values[bits] + edges - total)
        start = (1 - bits[0], 1 - bits[1], 1 - bits[2])
        piece = take_block(contribution, start, out_count)
        result = piece if result is None else result + piece
    return result * (scale / 12.0)


def diagonal_of(padded_moduli, scale):
    out_count = tuple((size - 2 for size in padded_moduli.shape[1:]))
    result = None
    for bits in offsets:
        piece = take_block(padded_moduli, (1 - bits[0], 1 - bits[1], 1 - bits[2]), out_count)
        result = piece if result is None else result + piece
    return result * (scale / 3.0)


def coarsen(moduli):
    shape = moduli.shape
    grouped = moduli.reshape(shape[0], shape[1] // 2, 2, shape[2] // 2, 2, shape[3] // 2, 2)
    return jnp.sum(grouped, axis=(2, 4, 6)) * 0.125


def restrict(padded):
    result = padded
    for axis in (1, 2, 3):
        core = result.shape[axis] - 2
        lower = lax.slice_in_dim(result, 0, core, 2, axis)
        middle = lax.slice_in_dim(result, 1, core + 1, 2, axis)
        upper = lax.slice_in_dim(result, 2, core + 2, 2, axis)
        result = middle + 0.5 * (lower + upper)
    return result


def prolong(padded):
    result = padded
    for axis in (1, 2, 3):
        core = result.shape[axis] - 2
        inner = lax.slice_in_dim(result, 1, core + 1, 1, axis)
        upper = lax.slice_in_dim(result, 2, core + 2, 1, axis)
        odd_nodes = 0.5 * (inner + upper)
        shape = list(inner.shape)
        shape[axis] = 2 * core
        result = jnp.stack([inner, odd_nodes], axis=axis + 1).reshape(shape)
    return result


def block_rims(array):
    return extended(array, (("gx", 1), ("gy", 2), ("gz", 3)), 1)


def extend(array):
    return block_rims(array)


def per_device(loads, density):
    moduli = (floor_modulus + (1.0 - floor_modulus) * (density * density * density))[None]
    source = loads
    saved = []
    current = None
    for section_no in range(LEVELS):
        scale = 2.0**section_no
        if section_no == LEVELS - 1:
            moduli_near = extend(moduli)
            diag_now = diagonal_of(moduli_near, scale)
            current = damping * source / diag_now
            for repeat in range(COARSE - 1):
                current = (
                    current
                    + damping
                    * (source - apply_stiffness(extend(current), moduli_near, scale))
                    / diag_now
                )
        else:
            moduli_near = extend(moduli)
            diag_now = diagonal_of(moduli_near, scale)
            current = damping * source / diag_now
            current = (
                current
                + damping
                * (source - apply_stiffness(extend(current), moduli_near, scale))
                / diag_now
            )
            residual = source - apply_stiffness(extend(current), moduli_near, scale)
            saved.append((current, (source, moduli_near, diag_now)))
            source = restrict(extend(residual))
            moduli = coarsen(moduli)
    for section_no in reversed(range(LEVELS - 1)):
        scale = 2.0**section_no
        correction = prolong(extend(current))
        kept, stored = saved[section_no]
        current = kept + correction
        source_now, moduli_near, diag_now = stored
        for repeat in range(SWEEPS):
            current = (
                current
                + damping
                * (source_now - apply_stiffness(extend(current), moduli_near, scale))
                / diag_now
            )
    return current


def solution(mesh):
    placed = (P(None, "gx", "gy", "gz"), P("gx", "gy", "gz"))
    return jax.shard_map(
        per_device, mesh=mesh, in_specs=placed, out_specs=P(None, "gx", "gy", "gz"), check_vma=False
    )
```

profile of v0, /device:TPU:1, one launch (start us, length us, event | category | flops | bytes accessed | tf_op | source)
XLA Modules:
  0.0 720.2 jit_solution(13158949827143605730)
XLA Ops:
  0.8 4.5 collective-permute-start
  5.3 5.6 collective-permute-start.1
  17.9 4.0 collective-permute-start.4
  38.3 4.0 collective-permute-done.8
  43.8 4.7 collective-permute-start.9
  64.3 4.9 collective-permute-start.13
  75.4 4.1 collective-permute-start.15
  80.8 4.1 collective-permute-start.25
  86.2 4.5 collective-permute-done.16
  97.7 5.2 collective-permute-start.27
  103.0 4.1 collective-permute-start.19
  111.7 5.3 collective-permute-start.21
  118.4 4.1 collective-permute-done.21
  122.5 4.8 collective-permute-done.22
  130.3 4.4 collective-permute-start.28
  153.3 3.8 collective-permute-done.33
  157.7 4.0 collective-permute-start.34
  188.1 5.5 collective-permute-start.40
  195.7 4.3 collective-permute-start.50
  200.0 4.3 collective-permute-start.42
  213.7 4.3 collective-permute-done.45
  219.7 5.9 collective-permute-start.51
  245.8 4.8 collective-permute-start.57
  284.1 4.0 collective-permute-start.65
  289.4 4.3 collective-permute-start.73
  302.5 7.1 collective-permute-start.74
  329.9 4.8 collective-permute-start.80
  355.7 4.2 collective-permute-start.86
  364.8 4.1 collective-permute-start.88
  381.3 4.8 collective-permute-start.92
  406.4 4.8 collective-permute-start.98
  431.1 4.8 collective-permute-start.104
  455.8 4.8 collective-permute-start.110
  480.5 4.8 collective-permute-start.116
  505.5 4.8 collective-permute-start.122
  530.4 4.8 collective-permute-start.128
  555.4 4.8 collective-permute-start.134
  580.7 4.8 collective-permute-start.140
  602.8 3.8 collective-permute-done.145
  607.2 4.0 collective-permute-start.146
  628.5 3.8 collective-permute-done.151
  632.8 4.0 collective-permute-start.152
  654.1 3.8 collective-permute-done.157
  659.7 4.0 collective-permute-start.158
  680.4 4.4 collective-permute-done.162
  684.8 3.9 collective-permute-done.163
  709.7 4.4 collective-permute-done.168
  714.2 3.9 collective-permute-done.169
  (567 shorter events, 499.6 us)
Async XLA Ops:
  0.8 10.1 %collective-permute-start = (f32[1,1,8,128]{3,2,1,0:T(8,128)S(1)}, f32[1,1,8,128]{3,2,1,0:T(8,128)S(1)}, u32[]{:S(2)}, u32[]{:S(2)}) collective-permute-start(f32[1,1,8,128]{3,2,1,0:T(8,128)S(1)} %get-tuple-element.212), channel_id=1, source_target_pairs={{0,64},{64,128},{128,192},{192,256},{256,320},{320,384},{384,448},... | collective-permute-start | bytes 12296 | tf_op jit(solution)/shard_map/ppermute | solution.py:24
  25.2 7.7 %collective-permute-start.5 = (f32[3,1,8,128]{3,2,1,0:T(8,128)S(1)}, f32[3,1,8,128]{3,2,1,0:T(8,128)S(1)}, u32[]{:S(2)}, u32[]{:S(2)}) collective-permute-start(f32[3,1,8,128]{3,2,1,0:T(8,128)S(1)} %get-tuple-element.109), channel_id=1, source_target_pairs={{0,64},{64,128},{128,192},{192,256},{256,320},{320,384},{384,448},... | collective-permute-start | bytes 36872 | tf_op jit(solution)/shard_map/ppermute | solution.py:24
  42.5 9.7 %collective-permute-start.10 = (f32[3,10,10,1]{3,2,1,0:T(8,128)S(1)}, f32[3,10,10,1]{3,2,1,0:T(8,128)S(1)}, u32[]{:S(2)}, u32[]{:S(2)}) collective-permute-start(f32[3,10,10,1]{3,2,1,0:T(8,128)S(1)} %get-tuple-element.60), channel_id=1, source_target_pairs={{1,0},{2,1},{3,2},{4,3},{5,4},{6,5},{7,6},{9,8},{10,9},{11,10},{12... | collective-permute-start | bytes 3608 | tf_op jit(solution)/shard_map/ppermute | solution.py:26
  43.8 10.2 %collective-permute-start.9 = (f32[3,10,10,1]{3,2,1,0:T(8,128)S(1)}, f32[3,10,10,1]{3,2,1,0:T(8,128)S(1)}, u32[]{:S(2)}, u32[]{:S(2)}) collective-permute-start(f32[3,10,10,1]{3,2,1,0:T(8,128)S(1)} %get-tuple-element.59), channel_id=1, source_target_pairs={{0,1},{1,2},{2,3},{3,4},{4,5},{5,6},{6,7},{8,9},{9,10},{10,11},{11... | collective-permute-start | bytes 3608 | tf_op jit(solution)/shard_map/ppermute | solution.py:24
  64.3 10.9 %collective-permute-start.13 = (f32[3,10,1,128]{3,2,1,0:T(1,128)S(1)}, f32[3,10,1,128]{3,2,1,0:T(1,128)S(1)}, u32[]{:S(2)}, u32[]{:S(2)}) collective-permute-start(f32[3,10,1,128]{3,2,1,0:T(1,128)S(1)} %get-tuple-element.95), channel_id=1, source_target_pairs={{0,8},{8,16},{16,24},{24,32},{32,40},{40,48},{48,56},{1,9},{9,17},... | collective-permute-start | bytes 46088 | tf_op jit(solution)/shard_map/ppermute | solution.py:24
  70.4 10.4 %collective-permute-start.23 = (f32[1,1,4,64]{3,2,1,0:T(4,128)S(1)}, f32[1,1,4,64]{3,2,1,0:T(4,128)S(1)}, u32[]{:S(2)}, u32[]{:S(2)}) collective-permute-start(f32[1,1,4,64]{3,2,1,0:T(4,128)S(1)} %get-tuple-element.385), channel_id=1, source_target_pairs={{0,64},{64,128},{128,192},{192,256},{256,320},{320,384},{384,448},... | collective-permute-start | bytes 3080 | tf_op jit(solution)/shard_map/ppermute | solution.py:24
  72.7 8.1 %collective-permute-start.24 = (f32[1,1,4,64]{3,2,1,0:T(4,128)S(1)}, f32[1,1,4,64]{3,2,1,0:T(4,128)S(1)}, u32[]{:S(2)}, u32[]{:S(2)}) collective-permute-start(f32[1,1,4,64]{3,2,1,0:T(4,128)S(1)} %get-tuple-element.386), channel_id=1, source_target_pairs={{64,0},{128,64},{192,128},{256,192},{320,256},{384,320},{448,384},... | collective-permute-start | bytes 3080 | tf_op jit(solution)/shard_map/ppermute | solution.py:26
  75.4 10.9 %collective-permute-start.15 = (f32[3,10,10,1]{3,2,1,0:T(8,128)S(1)}, f32[3,10,10,1]{3,2,1,0:T(8,128)S(1)}, u32[]{:S(2)}, u32[]{:S(2)}) collective-permute-start(f32[3,10,10,1]{3,2,1,0:T(8,128)S(1)} %get-tuple-element.57), channel_id=1, source_target_pairs={{0,1},{1,2},{2,3},{3,4},{4,5},{5,6},{6,7},{8,9},{9,10},{10,11},{11... | collective-permute-start | bytes 3608 | tf_op jit(solution)/shard_map/ppermute | solution.py:24
  79.5 11.2 %collective-permute-start.16 = (f32[3,10,10,1]{3,2,1,0:T(8,128)S(1)}, f32[3,10,10,1]{3,2,1,0:T(8,128)S(1)}, u32[]{:S(2)}, u32[]{:S(2)}) collective-permute-start(f32[3,10,10,1]{3,2,1,0:T(8,128)S(1)} %get-tuple-element.58), channel_id=1, source_target_pairs={{1,0},{2,1},{3,2},{4,3},{5,4},{6,5},{7,6},{9,8},{10,9},{11,10},{12... | collective-permute-start | bytes 3608 | tf_op jit(solution)/shard_map/ppermute | solution.py:26
  80.8 16.7 %collective-permute-start.25 = (f32[1,6,1,64]{3,2,1,0:T(1,128)S(1)}, f32[1,6,1,64]{3,2,1,0:T(1,128)S(1)}, u32[]{:S(2)}, u32[]{:S(2)}) collective-permute-start(f32[1,6,1,64]{3,2,1,0:T(1,128)S(1)} %get-tuple-element.381), channel_id=1, source_target_pairs={{0,8},{8,16},{16,24},{24,32},{32,40},{40,48},{48,56},{1,9},{9,17},... | collective-permute-start | bytes 4616 | tf_op jit(solution)/shard_map/ppermute | solution.py:24
  84.9 12.7 %collective-permute-start.26 = (f32[1,6,1,64]{3,2,1,0:T(1,128)S(1)}, f32[1,6,1,64]{3,2,1,0:T(1,128)S(1)}, u32[]{:S(2)}, u32[]{:S(2)}) collective-permute-start(f32[1,6,1,64]{3,2,1,0:T(1,128)S(1)} %get-tuple-element.382), channel_id=1, source_target_pairs={{8,0},{16,8},{24,16},{32,24},{40,32},{48,40},{56,48},{9,1},{17,9},... | collective-permute-start | bytes 4616 | tf_op jit(solution)/shard_map/ppermute | solution.py:26
  92.2 10.7 %collective-permute-start.17 = (f32[3,1,8,128]{3,2,1,0:T(8,128)S(1)}, f32[3,1,8,128]{3,2,1,0:T(8,128)S(1)}, u32[]{:S(2)}, u32[]{:S(2)}) collective-permute-start(f32[3,1,8,128]{3,2,1,0:T(8,128)S(1)} %get-tuple-element.105), channel_id=1, source_target_pairs={{0,64},{64,128},{128,192},{192,256},{256,320},{320,384},{384,448},... | collective-permute-start | bytes 36872 | tf_op jit(solution)/shard_map/ppermute | solution.py:24
  95.6 7.3 %collective-permute-start.18 = (f32[3,1,8,128]{3,2,1,0:T(8,128)S(1)}, f32[3,1,8,128]{3,2,1,0:T(8,128)S(1)}, u32[]{:S(2)}, u32[]{:S(2)}) collective-permute-start(f32[3,1,8,128]{3,2,1,0:T(8,128)S(1)} %get-tuple-element.106), channel_id=1, source_target_pairs={{64,0},{128,64},{192,128},{256,192},{320,256},{384,320},{448,384},... | collective-permute-start | bytes 36872 | tf_op jit(solution)/shard_map/ppermute | solution.py:26
  97.7 10.7 %collective-permute-start.27 = (f32[1,6,6,1]{3,2,1,0:T(8,128)S(1)}, f32[1,6,6,1]{3,2,1,0:T(8,128)S(1)}, u32[]{:S(2)}, u32[]{:S(2)}) collective-permute-start(f32[1,6,6,1]{3,2,1,0:T(8,128)S(1)} %pad_maximum_fusion.34), channel_id=1, source_target_pairs={{0,1},{1,2},{2,3},{3,4},{4,5},{5,6},{6,7},{8,9},{9,10},{10,11},{11... | collective-permute-start | bytes 440 | tf_op jit(solution)/shard_map/ppermute | solution.py:24
  111.7 10.8 %collective-permute-start.21 = (f32[3,10,10,1]{3,2,1,0:T(8,128)S(1)}, f32[3,10,10,1]{3,2,1,0:T(8,128)S(1)}, u32[]{:S(2)}, u32[]{:S(2)}) collective-permute-start(f32[3,10,10,1]{3,2,1,0:T(8,128)S(1)} %get-tuple-element.55), channel_id=1, source_target_pairs={{0,1},{1,2},{2,3},{3,4},{4,5},{5,6},{6,7},{8,9},{9,10},{10,11},{11... | collective-permute-start | bytes 3608 | tf_op jit(solution)/shard_map/ppermute | solution.py:24
  117.1 10.2 %collective-permute-start.22 = (f32[3,10,10,1]{3,2,1,0:T(8,128)S(1)}, f32[3,10,10,1]{3,2,1,0:T(8,128)S(1)}, u32[]{:S(2)}, u32[]{:S(2)}) collective-permute-start(f32[3,10,10,1]{3,2,1,0:T(8,128)S(1)} %get-tuple-element.56), channel_id=1, source_target_pairs={{1,0},{2,1},{3,2},{4,3},{5,4},{6,5},{7,6},{9,8},{10,9},{11,10},{12... | collective-permute-start | bytes 3608 | tf_op jit(solution)/shard_map/ppermute | solution.py:26
  157.7 11.6 %collective-permute-start.34 = (f32[3,1,4,64]{3,2,1,0:T(4,128)S(1)}, f32[3,1,4,64]{3,2,1,0:T(4,128)S(1)}, u32[]{:S(2)}, u32[]{:S(2)}) collective-permute-start(f32[3,1,4,64]{3,2,1,0:T(4,128)S(1)} %get-tuple-element.276), channel_id=1, source_target_pairs={{0,64},{64,128},{128,192},{192,256},{256,320},{320,384},{384,448},... | collective-permute-start | bytes 9224 | tf_op jit(solution)/shard_map/ppermute | solution.py:24
  161.7 7.5 %collective-permute-start.35 = (f32[3,1,4,64]{3,2,1,0:T(4,128)S(1)}, f32[3,1,4,64]{3,2,1,0:T(4,128)S(1)}, u32[]{:S(2)}, u32[]{:S(2)}) collective-permute-start(f32[3,1,4,64]{3,2,1,0:T(4,128)S(1)} %get-tuple-element.277), channel_id=1, source_target_pairs={{64,0},{128,64},{192,128},{256,192},{320,256},{384,320},{448,384},... | collective-permute-start | bytes 9224 | tf_op jit(solution)/shard_map/ppermute | solution.py:26
  163.6 10.7 %collective-permute-start.46 = (f32[1,1,2,32]{3,2,1,0:T(2,128)S(1)}, f32[1,1,2,32]{3,2,1,0:T(2,128)S(1)}, u32[]{:S(2)}, u32[]{:S(2)}) collective-permute-start(f32[1,1,2,32]{3,2,1,0:T(2,128)S(1)} %get-tuple-element.421), channel_id=1, source_target_pairs={{0,64},{64,128},{128,192},{192,256},{256,320},{320,384},{384,448},... | collective-permute-start | bytes 776 | tf_op jit(solution)/shard_map/ppermute | solution.py:24
  167.3 7.0 collective-permute-start.47
  177.8 9.6 %collective-permute-start.38 = (f32[3,6,6,1]{3,2,1,0:T(8,128)S(1)}, f32[3,6,6,1]{3,2,1,0:T(8,128)S(1)}, u32[]{:S(2)}, u32[]{:S(2)}) collective-permute-start(f32[3,6,6,1]{3,2,1,0:T(8,128)S(1)} %get-tuple-element.144), channel_id=1, source_target_pairs={{0,1},{1,2},{2,3},{3,4},{4,5},{5,6},{6,7},{8,9},{9,10},{10,11},{11... | collective-permute-start | bytes 1304 | tf_op jit(solution)/shard_map/ppermute | solution.py:24
  182.7 12.8 %collective-permute-start.48 = (f32[1,4,1,32]{3,2,1,0:T(1,128)S(1)}, f32[1,4,1,32]{3,2,1,0:T(1,128)S(1)}, u32[]{:S(2)}, u32[]{:S(2)}) collective-permute-start(f32[1,4,1,32]{3,2,1,0:T(1,128)S(1)} %get-tuple-element.409), channel_id=1, source_target_pairs={{0,8},{8,16},{16,24},{24,32},{32,40},{40,48},{48,56},{1,9},{9,17},... | collective-permute-start | bytes 1544 | tf_op jit(solution)/shard_map/ppermute | solution.py:24
  186.1 9.5 %collective-permute-start.49 = (f32[1,4,1,32]{3,2,1,0:T(1,128)S(1)}, f32[1,4,1,32]{3,2,1,0:T(1,128)S(1)}, u32[]{:S(2)}, u32[]{:S(2)}) collective-permute-start(f32[1,4,1,32]{3,2,1,0:T(1,128)S(1)} %get-tuple-element.410), channel_id=1, source_target_pairs={{8,0},{16,8},{24,16},{32,24},{40,32},{48,40},{56,48},{9,1},{17,9},... | collective-permute-start | bytes 1544 | tf_op jit(solution)/shard_map/ppermute | solution.py:26
  188.1 11.8 %collective-permute-start.40 = (f32[3,1,4,64]{3,2,1,0:T(4,128)S(1)}, f32[3,1,4,64]{3,2,1,0:T(4,128)S(1)}, u32[]{:S(2)}, u32[]{:S(2)}) collective-permute-start(f32[3,1,4,64]{3,2,1,0:T(4,128)S(1)} %get-tuple-element.274), channel_id=1, source_target_pairs={{0,64},{64,128},{128,192},{192,256},{256,320},{320,384},{384,448},... | collective-permute-start | bytes 9224 | tf_op jit(solution)/shard_map/ppermute | solution.py:24
  195.7 9.9 %collective-permute-start.50 = (f32[1,4,4,1]{3,2,1,0:T(4,128)S(1)}, f32[1,4,4,1]{3,2,1,0:T(4,128)S(1)}, u32[]{:S(2)}, u32[]{:S(2)}) collective-permute-start(f32[1,4,4,1]{3,2,1,0:T(4,128)S(1)} %pad_maximum_fusion.106), channel_id=1, source_target_pairs={{0,1},{1,2},{2,3},{3,4},{4,5},{5,6},{6,7},{8,9},{9,10},{10,11},{11... | collective-permute-start | bytes 200 | tf_op jit(solution)/shard_map/ppermute | solution.py:24
  219.7 7.8 %collective-permute-start.51 = (f32[3,1,2,32]{3,2,1,0:T(2,128)S(1)}, f32[3,1,2,32]{3,2,1,0:T(2,128)S(1)}, u32[]{:S(2)}, u32[]{:S(2)}) collective-permute-start(f32[3,1,2,32]{3,2,1,0:T(2,128)S(1)} %get-tuple-element.407), channel_id=1, source_target_pairs={{0,64},{64,128},{128,192},{192,256},{256,320},{320,384},{384,448},... | collective-permute-start | bytes 2312 | tf_op jit(solution)/shard_map/ppermute | solution.py:24
  245.8 6.9 collective-permute-start.57
  263.6 9.5 %collective-permute-start.61 = (f32[3,4,4,1]{3,2,1,0:T(4,128)S(1)}, f32[3,4,4,1]{3,2,1,0:T(4,128)S(1)}, u32[]{:S(2)}, u32[]{:S(2)}) collective-permute-start(f32[3,4,4,1]{3,2,1,0:T(4,128)S(1)} %get-tuple-element.261), channel_id=1, source_target_pairs={{0,1},{1,2},{2,3},{3,4},{4,5},{5,6},{6,7},{8,9},{9,10},{10,11},{11... | collective-permute-start | bytes 584 | tf_op jit(solution)/shard_map/ppermute | solution.py:24
  267.7 11.3 %collective-permute-start.69 = (f32[1,1,1,16]{3,2,1,0:T(1,128)S(1)}, f32[1,1,1,16]{3,2,1,0:T(1,128)S(1)}, u32[]{:S(2)}, u32[]{:S(2)}) collective-permute-start(f32[1,1,1,16]{3,2,1,0:T(1,128)S(1)} %multiply_bitcast_fusion.1), channel_id=1, source_target_pairs={{0,64},{64,128},{128,192},{192,256},{256,320},{320,384},{384,448},... | collective-permute-start | bytes 200 | tf_op jit(solution)/shard_map/ppermute | solution.py:24
  271.1 7.9 %collective-permute-start.70 = (f32[1,1,1,16]{3,2,1,0:T(1,128)S(1)}, f32[1,1,1,16]{3,2,1,0:T(1,128)S(1)}, u32[]{:S(2)}, u32[]{:S(2)}) collective-permute-start(f32[1,1,1,16]{3,2,1,0:T(1,128)S(1)} %multiply_bitcast_fusion.1), channel_id=1, source_target_pairs={{64,0},{128,64},{192,128},{256,192},{320,256},{384,320},{448,384},... | collective-permute-start | bytes 200 | tf_op jit(solution)/shard_map/ppermute | solution.py:26
  273.4 10.6 %collective-permute-start.63 = (f32[3,1,2,32]{3,2,1,0:T(2,128)S(1)}, f32[3,1,2,32]{3,2,1,0:T(2,128)S(1)}, u32[]{:S(2)}, u32[]{:S(2)}) collective-permute-start(f32[3,1,2,32]{3,2,1,0:T(2,128)S(1)} %get-tuple-element.395), channel_id=1, source_target_pairs={{0,64},{64,128},{128,192},{192,256},{256,320},{320,384},{384,448},... | collective-permute-start | bytes 2312 | tf_op jit(solution)/shard_map/ppermute | solution.py:24
  277.1 6.9 collective-permute-start.64
  279.1 10.3 %collective-permute-start.71 = (f32[1,3,1,16]{3,2,1,0:T(1,128)S(1)}, f32[1,3,1,16]{3,2,1,0:T(1,128)S(1)}, u32[]{:S(2)}, u32[]{:S(2)}) collective-permute-start(f32[1,3,1,16]{3,2,1,0:T(1,128)S(1)} %pad_maximum_fusion.155), channel_id=1, source_target_pairs={{0,8},{8,16},{16,24},{24,32},{32,40},{40,48},{48,56},{1,9},{9,17},... | collective-permute-start | bytes 584 | tf_op jit(solution)/shard_map/ppermute | solution.py:24
  284.1 9.7 %collective-permute-start.65 = (f32[3,4,1,32]{3,2,1,0:T(1,128)S(1)}, f32[3,4,1,32]{3,2,1,0:T(1,128)S(1)}, u32[]{:S(2)}, u32[]{:S(2)}) collective-permute-start(f32[3,4,1,32]{3,2,1,0:T(1,128)S(1)} %get-tuple-element.375), channel_id=1, source_target_pairs={{0,8},{8,16},{16,24},{24,32},{32,40},{40,48},{48,56},{1,9},{9,17},... | collective-permute-start | bytes 4616 | tf_op jit(solution)/shard_map/ppermute | solution.py:24
  289.4 8.7 %collective-permute-start.73 = (f32[1,3,3,1]{3,2,1,0:T(4,128)S(1)}, f32[1,3,3,1]{3,2,1,0:T(4,128)S(1)}, u32[]{:S(2)}, u32[]{:S(2)}) collective-permute-start(f32[1,3,3,1]{3,2,1,0:T(4,128)S(1)} %pad_maximum_fusion.121), channel_id=1, source_target_pairs={{0,1},{1,2},{2,3},{3,4},{4,5},{5,6},{6,7},{8,9},{9,10},{10,11},{11... | collective-permute-start | bytes 116 | tf_op jit(solution)/shard_map/ppermute | solution.py:24
  302.5 9.0 %collective-permute-start.74 = (f32[3,1,1,16]{3,2,1,0:T(1,128)S(1)}, f32[3,1,1,16]{3,2,1,0:T(1,128)S(1)}, u32[]{:S(2)}, u32[]{:S(2)}) collective-permute-start(f32[3,1,1,16]{3,2,1,0:T(1,128)S(1)} %get-tuple-element.5), channel_id=1, source_target_pairs={{0,64},{64,128},{128,192},{192,256},{256,320},{320,384},{384,448},... | collective-permute-start | bytes 584 | tf_op jit(solution)/shard_map/ppermute | solution.py:24
  329.9 6.7 collective-permute-start.80
  381.3 6.7 collective-permute-start.92
  406.4 6.7 collective-permute-start.98
  431.1 6.7 collective-permute-start.104
  455.8 6.7 collective-permute-start.110
  480.5 6.7 collective-permute-start.116
  505.5 6.7 collective-permute-start.122
  530.4 6.7 collective-permute-start.128
  676.2 8.6 %collective-permute-start.162 = (f32[3,10,10,1]{3,2,1,0:T(8,128)S(1)}, f32[3,10,10,1]{3,2,1,0:T(8,128)S(1)}, u32[]{:S(2)}, u32[]{:S(2)}) collective-permute-start(f32[3,10,10,1]{3,2,1,0:T(8,128)S(1)} %get-tuple-element.53), channel_id=1, source_target_pairs={{0,1},{1,2},{2,3},{3,4},{4,5},{5,6},{6,7},{8,9},{9,10},{10,11},{11... | collective-permute-start | bytes 3608 | tf_op jit(solution)/shard_map/ppermute | solution.py:24
  679.1 9.6 %collective-permute-start.163 = (f32[3,10,10,1]{3,2,1,0:T(8,128)S(1)}, f32[3,10,10,1]{3,2,1,0:T(8,128)S(1)}, u32[]{:S(2)}, u32[]{:S(2)}) collective-permute-start(f32[3,10,10,1]{3,2,1,0:T(8,128)S(1)} %get-tuple-element.54), channel_id=1, source_target_pairs={{1,0},{2,1},{3,2},{4,3},{5,4},{6,5},{7,6},{9,8},{10,9},{11,10},{12... | collective-permute-start | bytes 3608 | tf_op jit(solution)/shard_map/ppermute | solution.py:26
  705.6 8.6 %collective-permute-start.168 = (f32[3,10,10,1]{3,2,1,0:T(8,128)S(1)}, f32[3,10,10,1]{3,2,1,0:T(8,128)S(1)}, u32[]{:S(2)}, u32[]{:S(2)}) collective-permute-start(f32[3,10,10,1]{3,2,1,0:T(8,128)S(1)} %get-tuple-element.51), channel_id=1, source_target_pairs={{0,1},{1,2},{2,3},{3,4},{4,5},{5,6},{6,7},{8,9},{9,10},{10,11},{11... | collective-permute-start | bytes 3608 | tf_op jit(solution)/shard_map/ppermute | solution.py:24
  708.4 9.6 %collective-permute-start.169 = (f32[3,10,10,1]{3,2,1,0:T(8,128)S(1)}, f32[3,10,10,1]{3,2,1,0:T(8,128)S(1)}, u32[]{:S(2)}, u32[]{:S(2)}) collective-permute-start(f32[3,10,10,1]{3,2,1,0:T(8,128)S(1)} %get-tuple-element.52), channel_id=1, source_target_pairs={{1,0},{2,1},{3,2},{4,3},{5,4},{6,5},{7,6},{9,8},{10,9},{11,10},{12... | collective-permute-start | bytes 3608 | tf_op jit(solution)/shard_map/ppermute | solution.py:26
  (123 other events, 591.1 us)
where the time goes:
time: 725 us; the launch traced here: 720 us
  starting transfers between devices  447 us (62%)
  waiting for transfers between devices  239 us (33%)
  other arithmetic  17.5 us (2%)
  local copies, waits for them, and re-layouts  12.5 us (2%)
    ppermute x87, starting transfers between devices, extended(): lax.ppermute(tail, axis, [(i, (i + 1) % count) for i in range(ends)])  318 us
    ppermute x83, waiting for transfers between devices, extended(): lax.ppermute(head, axis, [((i + 1) % count, i) for i in range(ends)])  219 us
    ppermute x83, starting transfers between devices, extended(): lax.ppermute(head, axis, [((i + 1) % count, i) for i in range(ends)])  130 us
    ppermute x87, waiting for transfers between devices, extended(): lax.ppermute(tail, axis, [(i, (i + 1) % count) for i in range(ends)])  20.2 us
  transfers between devices with their start and end apart: 170, of which 80 were waited for; matrix products, arithmetic and copies ran while one was open for 1% of the time, Pallas kernels for 0%

commit v1 on v0

v1 whole, which is shorter than its diff:
```python
import functools
import itertools

import jax
import jax.numpy as jnp
from jax import lax
from jax.experimental import pallas as pl
from jax.experimental.pallas import tpu as pltpu
from jax.sharding import PartitionSpec as P

MESH = pl.DeviceIdType.MESH
F32 = jnp.float32
TILE = (8, 128)
SIDE = 8
ZHALO = 12
RING = (1, 2, 3, 4, -3, -2, -1)
XY8 = [(dx, dy) for dx in (-1, 0, 1) for dy in (-1, 0, 1) if dx or dy]
YZ23 = [(dy, dz) for dy in (0,) + RING for dz in (-1, 0, 1) if dy or dz]


def device(dx, dy, dz):
    return tuple(
        lax.rem(lax.axis_index(axis) + (step + SIDE), SIDE)
        for axis, step in (("gx", dx), ("gy", dy), ("gz", dz))
    )


def lanes():
    return lax.broadcasted_iota(jnp.int32, TILE, 1)


def rows():
    return lax.broadcasted_iota(jnp.int32, TILE, 0)


def up_plain(tile):
    return pltpu.roll(tile, 127, 1)


def down_plain(tile):
    return pltpu.roll(tile, 1, 1)


def up_pair(tile):
    turned = pltpu.roll(tile, 127, 1)
    return jnp.where(lanes() == 127, pltpu.roll(turned, 4, 0), turned)


def down_pair(tile):
    turned = pltpu.roll(tile, 1, 1)
    return jnp.where(lanes() == 0, pltpu.roll(turned, 4, 0), turned)


def twice(tile):
    return jnp.concatenate([tile, tile], axis=0)


def stencil(v, vp, m, ix, ys, mx, my, down):
    def column(y):
        held = {}
        for sx in (-1, 0, 1):
            a, b = v[ix + sx, y], vp[ix + sx, y]
            held[sx] = (a, b, a + b if sx else None)
        return held

    before, here = column(ys[0] - 1), column(ys[0])
    m_before = [m[mx - 1, ys[0] + my - 1], m[mx, ys[0] + my - 1]]
    for y in ys:
        after = column(y + 1)
        m_here = [m[mx - 1, y + my], m[mx, y + my]]
        above, below = None, None
        for sy, side, element in ((-1, before, m_before), (1, after, m_here)):
            for sx in (-1, 1):
                weight = element[0] if sx < 0 else element[1]
                both = side[sx][2]
                hi = weight * (both + (here[sx][1] + side[0][1]))
                lo = weight * (both + (here[sx][0] + side[0][0]))
                above = hi if above is None else above + hi
                below = lo if below is None else below + lo
        yield y, above + down(below)
        before, here, m_before = here, after, m_here


def loop(lower, upper, body):
    def step(i, carry):
        body(i)
        return carry

    lax.fori_loop(lower, upper, step, 0)


def diagonal(m, d4, inv, g, v, vp, xs, ys, up, down):
    def body(x):
        for y in ys:
            four = (m[x - 1, y - 1] + m[x - 1, y]) + (m[x, y - 1] + m[x, y])
            total = four + down(four)
            share = jnp.where(m[x, y] > 0.0, 0.15 / total, 0.0)
            d4[x, y] = 4.0 * total
            inv[x, y] = share
            first = share * g[x, y]
            v[x, y] = first
            vp[x, y] = up(first)

    loop(xs[0], xs[1], body)


def smooth(v, vp, m, inv, g, out, outp, xs, ys, up, down):
    def body(x):
        for y, around in stencil(v, vp, m, x, ys, x, 0, down):
            new = 0.4 * v[x, y] + inv[x, y] * (g[x, y] + around)
            out[x, y] = new
            outp[x, y] = up(new)

    loop(xs[0], xs[1], body)


def residual(v, vp, m, d4, g, out, xs, ys, down):
    def body(x):
        for y, around in stencil(v, vp, m, x, ys, x, 0, down):
            out[x, y] = (g[x, y] - d4[x, y] * v[x, y]) + around

    loop(xs[0], xs[1], body)


def restrict_xy(res, out, base, count):
    def body(i):
        x = base + 2 * i
        line = [
            res[x, y] + 0.5 * (res[x - 1, y] + res[x + 1, y])
            for y in range(base - 1, base + 2 * count)
        ]
        for k in range(count):
            out[i, k] = line[2 * k + 1] + 0.5 * (line[2 * k] + line[2 * k + 2])

    loop(0, count, body)


def coarsen_xy(m, out, base, count):
    def body(i):
        x = base + 2 * i
        for k in range(count):
            y = base + 2 * k
            out[i, k] = (m[x, y] + m[x, y + 1]) + (m[x + 1, y] + m[x + 1, y + 1])

    loop(0, count, body)


def place(index, own):
    if own == "all":
        return index
    if own == "beyond":
        return jnp.where(index < 64, index + 128, index - 128)
    return jnp.where(index < 96, index, index - 128)


def restriction(fine):
    f = place(lax.broadcasted_iota(jnp.int32, (128, 128), 0), fine)
    c = place(lax.broadcasted_iota(jnp.int32, (128, 128), 1), "round")
    gap = f - 2 * c
    return jnp.where(gap == 0, 0.5, jnp.where((gap == 1) | (gap == -1), 0.25, 0.0)).astype(F32)


def coarsening(fine):
    f = place(lax.broadcasted_iota(jnp.int32, (128, 128), 0), fine)
    c = place(lax.broadcasted_iota(jnp.int32, (128, 128), 1), "round")
    gap = f - 2 * c
    return jnp.where((gap == 0) | (gap == 1), 0.125, 0.0).astype(F32)


def prolongation(fine):
    c = place(lax.broadcasted_iota(jnp.int32, (128, 128), 0), "round")
    f = place(lax.broadcasted_iota(jnp.int32, (128, 128), 1), fine)
    gap = f - 2 * c
    return jnp.where(gap == 0, 1.0, jnp.where((gap == 1) | (gap == -1), 0.5, 0.0)).astype(F32)


def product(a, b):
    return jnp.dot(a, b, precision=lax.Precision.HIGHEST, preferred_element_type=F32)


def rise(source, mats, before, m, inv, g, zs, c, cp, a, ap, out, up, down):
    flat = source.reshape(7 * 7 * 8, 128)
    spread = product(flat, mats[0])
    if len(mats) == 2:
        top = lax.broadcasted_iota(jnp.int32, (7 * 7 * 8, 128), 0) % 8 < 4
        spread = jnp.where(top, spread, product(flat, mats[1]))
    zs[...] = spread.reshape(7, 7, 8, 128)
    m_ref, mx, my = m
    i_ref, ix, iy = inv
    g_ref, gx, gy = g

    def correct(i):
        for half in (0, 1):
            x = 2 * i + half
            line = [zs[i, k] if half == 0 else 0.5 * (zs[i, k] + zs[i + 1, k]) for k in range(7)]
            for y in range(12):
                k = y // 2
                add = line[k] if y % 2 == 0 else 0.5 * (line[k] + line[k + 1])
                new = jnp.where(m_ref[x + mx, y + my] > 0.0, before(x, y) + add, 0.0)
                c[x, y] = new
                cp[x, y] = up(new)

    loop(0, 6, correct)

    def sweep_a(x):
        for y, around in stencil(c, cp, m_ref, x, range(1, 11), x + mx, my, down):
            new = 0.4 * c[x, y] + i_ref[x + ix, y + iy] * (g_ref[x + gx, y + gy] + around)
            new = jnp.where(m_ref[x + mx, y + my] > 0.0, new, 0.0)
            a[x, y] = new
            ap[x, y] = up(new)

    loop(1, 11, sweep_a)

    def sweep_b(x):
        for y, around in stencil(a, ap, m_ref, x, range(2, 10), x + mx, my, down):
            new = 0.4 * a[x, y] + i_ref[x + ix, y + iy] * (g_ref[x + gx, y + gy] + around)
            new = jnp.where(m_ref[x + mx, y + my] > 0.0, new, 0.0)
            out(x - 2, y - 2, new)

    loop(2, 10, sweep_b)


def kernel(
    block, out, e0, zsend, zrecv, g0, m0, d0, i0, v0, vp0, u0, up0, r0,
    t1, tm1, e1, u1x, g1, m1, d1, i1, v1, vp1, u1, up1, r1,
    t2, tm2, yz, x2, g2, m2, d2, i2, v2, vp2, u2, up2, r2,
    t3, tm3, g3, m3, d3, i3, v3, vp3, u3, up3,
    zs, c, cp, a, ap, f2, f1,
    s0, q0, s1, q1, s1u, q1u, sy, qy, sx, qx,
):
    gx, gy, gz = (lax.axis_index(axis) for axis in ("gx", "gy", "gz"))

    partners = {(dx, dy, dz) for dx in (-1, 0, 1) for dy in (-1, 0, 1) for dz in (-1, 0, 1)}
    partners |= {(0, dy, dz) for dy, dz in YZ23} | {(dx, 0, 0) for dx in RING}
    partners = sorted(partners - {(0, 0, 0)})
    barrier = pltpu.get_barrier_semaphore()
    for o in partners:
        pl.semaphore_signal(barrier, inc=1, device_id=device(*o), device_id_type=MESH)

    for x in range(8):
        for y in range(0, 8, 2):
            pair = block[pl.ds((x * 8 + y) * 4, 8), :]
            e0[x + 4, y + 4] = pair[0:4]
            e0[x + 4, y + 5] = pair[4:8]
    k16 = lax.broadcasted_iota(jnp.int32, (16, 128), 0)
    l16 = lax.broadcasted_iota(jnp.int32, (16, 128), 1)
    pick_low = jnp.where((l16 == 128 - ZHALO + k16) & (k16 < ZHALO), 1.0, 0.0).astype(F32)
    pick_high = jnp.where((l16 == k16) & (k16 < ZHALO), 1.0, 0.0).astype(F32)
    for side, pick in enumerate((pick_low, pick_high)):
        for half in (0, 1):
            zsend[side, half] = lax.dot_general(
                pick, block[pl.ds(half * 128, 128), :], (((1,), (1,)), ((), ())),
                precision=lax.Precision.HIGHEST, preferred_element_type=F32,
            )

    zero = jnp.zeros(TILE, F32)

    def rim2(x):
        for y in range(28):
            m2[x, y] = zero

    loop(0, 28, rim2)
    for ref in (v2, vp2, u2, up2, r2):
        for i in range(5, 23):
            for j in (5, 22):
                ref[i, j] = zero
                ref[j, i] = zero

    def rim3(x):
        for y in range(16):
            for ref in (m3, v3, vp3, u3, up3):
                ref[x, y] = zero

    loop(0, 16, rim3)
    pl.semaphore_wait(barrier, len(partners))

    span = {-1: (4, 12, 3), 0: (4, 4, 8), 1: (8, 0, 4)}
    copies = []
    for n, (dx, dy) in enumerate(XY8):
        (ax, bx, cx), (ay, by, cy) = span[dx], span[dy]
        copies.append(
            pltpu.make_async_remote_copy(
                src_ref=e0.at[pl.ds(ax, cx), pl.ds(ay, cy)],
                dst_ref=e0.at[pl.ds(bx, cx), pl.ds(by, cy)],
                send_sem=s0.at[n], recv_sem=q0.at[n],
                device_id=device(dx, dy, 0), device_id_type=MESH,
            )
        )
    n = 8
    for dz in (-1, 1):
        side = 0 if dz > 0 else 1
        for dx, dy in itertools.product((-1, 0, 1), repeat=2):
            first, count = {-1: (0, 1), 0: (0, 2), 1: (1, 1)}[dx]
            copies.append(
                pltpu.make_async_remote_copy(
                    src_ref=zsend.at[side, pl.ds(first, count)],
                    dst_ref=zrecv.at[side, 1 - dx, 1 - dy, pl.ds(first, count)],
                    send_sem=s0.at[n], recv_sem=q0.at[n],
                    device_id=device(dx, dy, dz), device_id_type=MESH,
                )
            )
            n += 1
    for copy in copies:
        copy.start()
    for copy in copies:
        copy.wait()

    top = rows() < 4
    lane = lanes()
    beyond_ok = ((lane < ZHALO) & (gz < SIDE - 1)) | ((lane >= 128 - ZHALO) & (gz > 0))
    known = top | beyond_ok
    put = jnp.concatenate([pick_low, pick_high], axis=0)
    for rx, ry in itertools.product((-1, 0, 1), repeat=2):
        x_from, x_to = {-1: (-4, 0), 0: (0, 8), 1: (8, 11)}[rx]
        y_from, y_to = {-1: (-4, 0), 0: (0, 8), 1: (8, 11)}[ry]
        inside = None
        if rx:
            inside = gx > 0 if rx < 0 else gx < SIDE - 1
        if ry:
            more = gy > 0 if ry < 0 else gy < SIDE - 1
            inside = more if inside is None else inside & more
        ok = known if inside is None else known & inside
        for half in {-1: (1,), 0: (0, 1), 1: (0,)}[rx]:
            both = jnp.concatenate([zrecv[0, rx + 1, ry + 1, half], zrecv[1, rx + 1, ry + 1, half]], axis=0)
            ends = lax.dot_general(
                both, put, (((0,), (0,)), ((), ())),
                precision=lax.Precision.HIGHEST, preferred_element_type=F32,
            )
            for x in range(x_from, x_to):
                source_x = x % 8
                if source_x // 4 != half:
                    continue
                for y in range(y_from, y_to):
                    at = ((source_x % 4) * 8 + y % 8) * 4
                    held = ends[at // 8 * 8 : at // 8 * 8 + 8]
                    if at % 8 == 0:
                        held = pltpu.roll(held, 4, 0)
                    own = e0[x + 4, y + 4]
                    whole = jnp.where(top, twice(own), held)
                    dens = jnp.where(top, jnp.broadcast_to(whole[3:4], TILE), jnp.broadcast_to(whole[7:8], TILE))
                    g0[x + 4, y + 4] = jnp.where(ok, 1.8 * whole, 0.0)
                    m0[x + 4, y + 4] = jnp.where(
                        ok, 0.15 * (0.001 + (1.0 - 0.001) * (dens * dens * dens)), 0.0
                    )

    diagonal(m0, d0, i0, g0, v0, vp0, (1, 15), range(1, 15), up_pair, down_pair)
    smooth(v0, vp0, m0, i0, g0, u0, up0, (2, 14), range(2, 14), up_pair, down_pair)
    residual(u0, up0, m0, d0, g0, r0, (3, 12), range(3, 12), down_pair)
    restrict_xy(r0, t1, 4, 4)
    coarsen_xy(m0, tm1, 4, 4)
    top128 = lax.broadcasted_iota(jnp.int32, (128, 128), 0) % 8 < 4
    flat = t1[...].reshape(128, 128)
    new_g = jnp.where(top128, product(flat, restriction("all")), product(flat, restriction("beyond")))
    flat = tm1[...].reshape(128, 128)
    new_m = jnp.where(top128, product(flat, coarsening("all")), product(flat, coarsening("beyond")))
    for x in range(4):
        for y in range(4):
            at = (x * 4 + y) * 8
            tg = new_g[at : at + 8]
            tm = new_m[at : at + 8]
            tg = tg + pltpu.roll(tg, 4, 0)
            tm = tm + pltpu.roll(tm, 4, 0)
            e1[x + 4, y + 4] = jnp.where(rows() == 3, tm, tg)[0:4]

    def blocks8(ref, send, recv):
        found = []
        for n, (dx, dy) in enumerate(XY8):
            found.append(
                pltpu.make_async_remote_copy(
                    src_ref=ref.at[pl.ds(4, 4), pl.ds(4, 4)],
                    dst_ref=ref.at[pl.ds({-1: 8, 0: 4, 1: 0}[dx], 4), pl.ds({-1: 8, 0: 4, 1: 0}[dy], 4)],
                    send_sem=send.at[n], recv_sem=recv.at[n],
                    device_id=device(dx, dy, 0), device_id_type=MESH,
                )
            )
        return found

    copies = blocks8(e1, s1, q1)
    for copy in copies:
        copy.start()
    for copy in copies:
        copy.wait()

    def take1(x):
        inside_x = jnp.where(((x >= 4) | (gx > 0)) & ((x < 8) | (gx < SIDE - 1)), 1.0, 0.0)
        for y in range(12):
            factor = inside_x
            if y < 4:
                factor = factor * jnp.where(gy > 0, 1.0, 0.0)
            if y >= 8:
                factor = factor * jnp.where(gy < SIDE - 1, 1.0, 0.0)
            whole = twice(e1[x, y]) * factor
            mod = jnp.broadcast_to(whole[3:4], TILE)
            m1[x, y] = mod
            g1[x, y] = jnp.where(mod > 0.0, whole, 0.0)

    loop(0, 12, take1)
    diagonal(m1, d1, i1, g1, v1, vp1, (1, 12), range(1, 12), up_plain, down_plain)
    smooth(v1, vp1, m1, i1, g1, u1, up1, (2, 9), range(2, 9), up_plain, down_plain)
    for x in range(4):
        for y in range(4):
            u1x[x + 4, y + 4] = u1[x + 4, y + 4][0:4]
    u_copies = blocks8(u1x, s1u, q1u)
    residual(u1, up1, m1, d1, g1, r1, (3, 8), range(3, 8), down_plain)
    restrict_xy(r1, t2, 4, 2)
    coarsen_xy(m1, tm2, 4, 2)
    new_g = product(t2[...].reshape(32, 128), restriction("round"))
    new_m = product(tm2[...].reshape(32, 128), coarsening("round"))
    for x in range(2):
        for y in range(2):
            at = (x * 2 + y) * 8
            both = jnp.where(rows() == 3, new_m[at : at + 8], new_g[at : at + 8])
            both = jnp.where(lane < 32, both, 0.0)
            yz[1, x, 2 * gy + y] = both[0:4]

    copies = []
    for n, (dy, dz) in enumerate(YZ23):
        copies.append(
            pltpu.make_async_remote_copy(
                src_ref=yz.at[1, :, pl.ds(2 * gy, 2)],
                dst_ref=yz.at[1 - dz, :, pl.ds(2 * gy, 2)],
                send_sem=sy.at[n], recv_sem=qy.at[n],
                device_id=device(0, dy, dz), device_id_type=MESH,
            )
        )
    for copy in copies:
        copy.start()
    for copy in u_copies:
        copy.start()
    for copy in copies:
        copy.wait()
    low_ok = jnp.where(gz > 0, 1.0, 0.0)
    high_ok = jnp.where(gz < SIDE - 1, 1.0, 0.0)
    for x in range(2):
        for y in range(16):
            x2[2 * gx + x, y] = (
                yz[1, x, y]
                + pltpu.roll(yz[0, x, y], 96, 1) * low_ok
                + pltpu.roll(yz[2, x, y], 32, 1) * high_ok
            )

    copies = []
    for n, dx in enumerate(RING):
        copies.append(
            pltpu.make_async_remote_copy(
                src_ref=x2.at[pl.ds(2 * gx, 2)],
                dst_ref=x2.at[pl.ds(2 * gx, 2)],
                send_sem=sx.at[n], recv_sem=qx.at[n],
                device_id=device(dx, 0, 0), device_id_type=MESH,
            )
        )
    for copy in copies:
        copy.start()
    for copy in copies:
        copy.wait()

    def take2(x):
        for y in range(16):
            whole = twice(x2[x, y])
            mod = jnp.broadcast_to(whole[3:4], TILE)
            m2[x + 6, y + 6] = mod
            g2[x + 6, y + 6] = jnp.where(mod > 0.0, whole, 0.0)

    loop(0, 16, take2)
    diagonal(m2, d2, i2, g2, v2, vp2, (6, 22), range(6, 22), up_plain, down_plain)
    smooth(v2, vp2, m2, i2, g2, u2, up2, (6, 22), range(6, 22), up_plain, down_plain)
    residual(u2, up2, m2, d2, g2, r2, (6, 22), range(6, 22), down_plain)
    restrict_xy(r2, t3, 6, 8)
    coarsen_xy(m2, tm3, 6, 8)
    new_g = product(t3[...].reshape(512, 128), restriction("round")).reshape(8, 8, 8, 128)
    new_m = product(tm3[...].reshape(512, 128), coarsening("round")).reshape(8, 8, 8, 128)
    m3[pl.ds(4, 8), pl.ds(4, 8)] = new_m
    g3[pl.ds(4, 8), pl.ds(4, 8)] = jnp.where(new_m > 0.0, new_g, 0.0)

    diagonal(m3, d3, i3, g3, v3, vp3, (4, 12), range(4, 12), up_plain, down_plain)

    def two(i):
        smooth(v3, vp3, m3, i3, g3, u3, up3, (4, 12), range(4, 12), up_plain, down_plain)
        smooth(u3, up3, m3, i3, g3, v3, vp3, (4, 12), range(4, 12), up_plain, down_plain)

    loop(0, 3, two)
    smooth(v3, vp3, m3, i3, g3, u3, up3, (4, 12), range(4, 12), up_plain, down_plain)

    def keep(ref):
        def store(x, y, new):
            ref[x, y] = new

        return store

    x_at, y_at = 2 * gx + 2, 2 * gy + 2
    rise(
        u3[pl.ds(gx + 2, 7), pl.ds(gy + 2, 7)],
        (prolongation("round"),),
        lambda x, y: u2[x + x_at, y + y_at],
        (m2, x_at, y_at), (i2, x_at, y_at), (g2, x_at, y_at),
        zs, c, cp, a, ap, keep(f2), up_plain, down_plain,
    )
    for copy in u_copies:
        copy.wait()
    rise(
        f2[pl.ds(0, 7), pl.ds(0, 7)],
        (prolongation("round"),),
        lambda x, y: twice(u1x[x, y]),
        (m1, 0, 0), (i1, 0, 0), (g1, 0, 0),
        zs, c, cp, a, ap, keep(f1), up_plain, down_plain,
    )

    def finish(x, y, new):
        out[pl.ds(pl.multiple_of((x * 8 + y) * 8, 8), 8), :] = new

    rise(
        f1[pl.ds(1, 7), pl.ds(1, 7)],
        (prolongation("all"), prolongation("beyond")),
        lambda x, y: u0[x + 2, y + 2],
        (m0, 2, 2), (i0, 2, 2), (g0, 2, 2),
        zs, c, cp, a, ap, finish, up_pair, down_pair,
    )


def per_device(loads, density):
    block = jnp.concatenate([jnp.transpose(loads, (1, 2, 0, 3)), density[:, :, None]], axis=2)

    def tiles(*lead):
        return pltpu.VMEM(lead + TILE, F32)

    def thin(*lead):
        return pltpu.VMEM(lead + (4, 128), F32)

    sems = []
    for count in (26, 8, 8, 23, 7):
        sems += [pltpu.SemaphoreType.DMA((count,))] * 2
    result = pl.pallas_call(
        kernel,
        out_shape=jax.ShapeDtypeStruct((512, 128), F32),
        in_specs=[pl.BlockSpec(memory_space=pltpu.VMEM)],
        out_specs=pl.BlockSpec(memory_space=pltpu.VMEM),
        scratch_shapes=[thin(15, 15), pltpu.VMEM((2, 2, 16, 128), F32), pltpu.VMEM((2, 3, 3, 2, 16, 128), F32)]
        + [tiles(15, 15)] * 9
        + [tiles(4, 4)] * 2
        + [thin(12, 12)] * 2
        + [tiles(12, 12)] * 9
        + [tiles(2, 2)] * 2
        + [thin(3, 2, 16), thin(16, 16)]
        + [tiles(28, 28)] * 9
        + [tiles(8, 8)] * 2
        + [tiles(16, 16)] * 8
        + [tiles(7, 7)]
        + [tiles(12, 12)] * 4
        + [tiles(8, 8)] * 2
        + sems,
        compiler_params=pltpu.CompilerParams(
            collective_id=0, has_side_effects=True, vmem_limit_bytes=60 * 2**20
        ),
        cost_estimate=pl.CostEstimate(flops=10**8, bytes_accessed=10**6, transcendentals=0),
    )(block.reshape(256, 128))
    return jnp.transpose(result.reshape(8, 8, 8, 128)[:, :, :3], (2, 0, 1, 3))


def solution(mesh):
    placed = (P(None, "gx", "gy", "gz"), P("gx", "gy", "gz"))
    return jax.shard_map(
        per_device, mesh=mesh, in_specs=placed, out_specs=P(None, "gx", "gy", "gz"), check_vma=False
    )
```

time: 725 us -> 90.5 us (0.12)
  starting transfers between devices: 447 us -> 0 us
  waiting for transfers between devices: 239 us -> 0 us
  Pallas kernels: 0 us -> 87 us
  other arithmetic: 17.5 us -> 0.92 us
  local copies, waits for them, and re-layouts: 12.5 us -> 2.36 us
    ppermute x170 -> x0, starting transfers between devices: 447 us -> none  [the longest x87 318 us: extended(): lax.ppermute(tail, axis, [(i, (i + 1) % count) for i in range(ends)])]
    ppermute x170 -> x0, waiting for transfers between devices: 239 us -> none  [the longest x83 219 us: extended(): lax.ppermute(head, axis, [((i + 1) % count, i) for i in range(ends)])]
    pallas_call x0 -> x1, Pallas kernels: none -> 87 us  [per_device(): pl.pallas_call(kernel, out_shape=jax.ShapeDtypeStruct((512, 128), F32), i...]
    add x45 -> x0, other arithmetic: 8.41 us -> none  [the longest x6 2.75 us: per_device(): current + damping * (source_now - apply_stiffness(extend(current), moduli...]
  transfers between devices with their start and end apart: 170 -> 0, of which waited for: 80 -> 0; matrix products, arithmetic and copies ran while one was open for 1% -> 0% of each run, Pallas kernels for 0% -> 0%
where the time goes in v1:
time: 90.5 us; the launch traced here: 90.3 us
  Pallas kernels  87 us (96%)
  local copies, waits for them, and re-layouts  2.36 us (3%)
  other arithmetic  0.92 us (1%)
    pallas_call x1, Pallas kernels, per_device(): pl.pallas_call(kernel, out_shape=jax.ShapeDtypeStruct((512, 128), F32), i...  87 us

profile of v1, /device:TPU:1, one launch (start us, length us, event | category | flops | bytes accessed | tf_op | source)
XLA Modules:
  0.0 90.3 jit_solution(8979805303179285878)
XLA Ops:
  0.0 0.9 %pad_maximum_fusion = f32[8,8,4,128]{3,1,0,2:T(8,128)S(1)} fusion(f32[8,8,1,128]{3,1,0,2:T(8,128)} %bitcast.10, f32[8,8,3,128]{3,1,0,2:T(8,128)} %bitcast.9), kind=kLoop, calls=%fused_computation | loop fusion | flops 32768 | bytes 262144 | tf_op jit(solution)/shard_map/concatenate | solution.py:521
  0.9 0.7 copy.3
  1.7 87.0 %shard_map.28 = f32[512,128]{1,0:T(8,128)} custom-call(f32[256,128]{1,0:T(8,128)} %bitcast.8), custom_call_target="tpu_custom_call" | custom-call | flops 100000000 | bytes 1000000 | tf_op jit(solution)/shard_map/pallas_call | solution.py:532
  88.7 1.0 %slice.4 = f32[8,8,3,128]{3,2,1,0:T(4,128)S(1)} slice(f32[8,8,8,128]{3,2,1,0:T(8,128)} %bitcast.7), slice={[0:8], [0:8], [0:3], [0:128]} | slice | bytes 196608 | tf_op jit(solution)/shard_map/slice | solution.py:556
  89.7 0.6 copy.7

commit v2 on v1

v2 whole, which is shorter than its diff:
```python
import functools
import itertools

import jax
import jax.numpy as jnp
from jax import lax
from jax.experimental import pallas as pl
from jax.experimental.pallas import tpu as pltpu
from jax.sharding import PartitionSpec as P

MESH = pl.DeviceIdType.MESH
F32 = jnp.float32
TILE = (8, 128)
SIDE = 8
UNROLL = 8
ZHALO = 12
RING = (1, 2, 3, 4, -3, -2, -1)
XY8 = [(dx, dy) for dx in (-1, 0, 1) for dy in (-1, 0, 1) if dx or dy]
YZ23 = [(dy, dz) for dy in (0,) + RING for dz in (-1, 0, 1) if dy or dz]


def device(dx, dy, dz):
    return tuple(
        lax.rem(lax.axis_index(axis) + (step + SIDE), SIDE)
        for axis, step in (("gx", dx), ("gy", dy), ("gz", dz))
    )


def lanes(shape=TILE):
    return lax.broadcasted_iota(jnp.int32, shape, len(shape) - 1)


def rows(shape=TILE):
    return lax.broadcasted_iota(jnp.int32, shape, len(shape) - 2)


def turn_rows(tiles, by):
    return pltpu.roll(tiles, by, tiles.ndim - 2)


def turn_lanes(tiles, by):
    return pltpu.roll(tiles, by, tiles.ndim - 1)


def up_plain(tiles):
    return turn_lanes(tiles, 127)


def down_plain(tiles):
    return turn_lanes(tiles, 1)


def up_pair(tiles):
    turned = turn_lanes(tiles, 127)
    return jnp.where(lanes(tiles.shape) == 127, turn_rows(turned, 4), turned)


def down_pair(tiles):
    turned = turn_lanes(tiles, 1)
    return jnp.where(lanes(tiles.shape) == 0, turn_rows(turned, 4), turned)


def twice(tiles):
    return jnp.concatenate([tiles, tiles], axis=tiles.ndim - 2)


def spread(tiles, row):
    return jnp.broadcast_to(tiles[..., row : row + 1, :], tiles.shape)


def stencil(v, vp, m, ix, y0, n, mx, my, down):
    wide = pl.ds(y0 - 1, n + 2)
    lower = {sx: v[ix + sx, wide] for sx in (-1, 0, 1)}
    upper = {sx: vp[ix + sx, wide] for sx in (-1, 0, 1)}
    weights = {-1: m[mx - 1, pl.ds(y0 + my - 1, n + 1)], 1: m[mx, pl.ds(y0 + my - 1, n + 1)]}
    above, below = None, None
    for sx in (-1, 1):
        both = lower[sx] + upper[sx]
        for sy in (-1, 1):
            side = slice(1 + sy, 1 + sy + n)
            weight = weights[sx][0:n] if sy < 0 else weights[sx][1 : n + 1]
            hi = weight * (both[side] + (upper[sx][1 : n + 1] + upper[0][side]))
            lo = weight * (both[side] + (lower[sx][1 : n + 1] + lower[0][side]))
            above = hi if above is None else above + hi
            below = lo if below is None else below + lo
    return above + down(below)


def loop(lower, upper, body):
    count = upper - lower
    each = max(k for k in range(1, UNROLL + 1) if count % k == 0)

    def step(i, carry):
        for k in range(each):
            body(lower + i * each + k)
        return carry

    if each == count:
        step(0, 0)
    else:
        lax.fori_loop(0, count // each, step, 0)


def diagonal(m, d4, inv, g, v, vp, xs, ys, up, down):
    y0, n = ys
    at = pl.ds(y0, n)

    def body(x):
        pairs = m[x - 1, pl.ds(y0 - 1, n + 1)] + m[x, pl.ds(y0 - 1, n + 1)]
        four = pairs[0:n] + pairs[1 : n + 1]
        total = four + down(four)
        share = jnp.where(m[x, at] > 0.0, 0.15 / total, 0.0)
        d4[x, at] = 4.0 * total
        inv[x, at] = share
        first = share * g[x, at]
        v[x, at] = first
        vp[x, at] = up(first)

    loop(xs[0], xs[1], body)


def smooth(v, vp, m, inv, g, out, outp, xs, ys, up, down):
    y0, n = ys
    at = pl.ds(y0, n)

    def body(x):
        around = stencil(v, vp, m, x, y0, n, x, 0, down)
        new = 0.4 * v[x, at] + inv[x, at] * (g[x, at] + around)
        out[x, at] = new
        outp[x, at] = up(new)

    loop(xs[0], xs[1], body)


def residual(v, vp, m, d4, g, out, xs, ys, down):
    y0, n = ys
    at = pl.ds(y0, n)

    def body(x):
        around = stencil(v, vp, m, x, y0, n, x, 0, down)
        out[x, at] = (g[x, at] - d4[x, at] * v[x, at]) + around

    loop(xs[0], xs[1], body)


def restrict_xy(res, out, base, count):
    def body(i):
        x = base + 2 * i
        wide = pl.ds(base - 1, 2 * count + 1)
        line = res[x, wide] + 0.5 * (res[x - 1, wide] + res[x + 1, wide])
        for k in range(count):
            out[i, k] = line[2 * k + 1] + 0.5 * (line[2 * k] + line[2 * k + 2])

    loop(0, count, body)


def coarsen_xy(m, out, base, count):
    def body(i):
        x = base + 2 * i
        wide = pl.ds(base, 2 * count)
        line = m[x, wide] + m[x + 1, wide]
        for k in range(count):
            out[i, k] = line[2 * k] + line[2 * k + 1]

    loop(0, count, body)


def place(index, own):
    if own == "all":
        return index
    if own == "beyond":
        return jnp.where(index < 64, index + 128, index - 128)
    return jnp.where(index < 96, index, index - 128)


def restriction(fine):
    f = place(lax.broadcasted_iota(jnp.int32, (128, 128), 0), fine)
    c = place(lax.broadcasted_iota(jnp.int32, (128, 128), 1), "round")
    gap = f - 2 * c
    return jnp.where(gap == 0, 0.5, jnp.where((gap == 1) | (gap == -1), 0.25, 0.0)).astype(F32)


def coarsening(fine):
    f = place(lax.broadcasted_iota(jnp.int32, (128, 128), 0), fine)
    c = place(lax.broadcasted_iota(jnp.int32, (128, 128), 1), "round")
    gap = f - 2 * c
    return jnp.where((gap == 0) | (gap == 1), 0.125, 0.0).astype(F32)


def prolongation(fine):
    c = place(lax.broadcasted_iota(jnp.int32, (128, 128), 0), "round")
    f = place(lax.broadcasted_iota(jnp.int32, (128, 128), 1), fine)
    gap = f - 2 * c
    return jnp.where(gap == 0, 1.0, jnp.where((gap == 1) | (gap == -1), 0.5, 0.0)).astype(F32)


def product(a, b):
    return jnp.dot(a, b, precision=lax.Precision.HIGHEST, preferred_element_type=F32)


def rise(source, mats, before, m, inv, g, zs, c, cp, a, ap, out, up, down):
    flat = source.reshape(7 * 7 * 8, 128)
    wide = product(flat, mats[0])
    if len(mats) == 2:
        top = lax.broadcasted_iota(jnp.int32, (7 * 7 * 8, 128), 0) % 8 < 4
        wide = jnp.where(top, wide, product(flat, mats[1]))
    zs[...] = wide.reshape(7, 7, 8, 128)
    m_ref, mx, my = m
    i_ref, ix, iy = inv
    g_ref, gx, gy = g

    def correct(i):
        for half in (0, 1):
            x = 2 * i + half
            line = zs[i] if half == 0 else 0.5 * (zs[i] + zs[i + 1])
            middle = 0.5 * (line[0:6] + line[1:7])
            add = jnp.stack([line[0:6], middle], axis=1).reshape((12,) + TILE)
            new = jnp.where(m_ref[x + mx, pl.ds(my, 12)] > 0.0, before(x) + add, 0.0)
            c[x] = new
            cp[x] = up(new)

    loop(0, 6, correct)

    def sweep(old, oldp, x, y0, n):
        around = stencil(old, oldp, m_ref, x, y0, n, x + mx, my, down)
        new = 0.4 * old[x, pl.ds(y0, n)] + i_ref[x + ix, pl.ds(y0 + iy, n)] * (
            g_ref[x + gx, pl.ds(y0 + gy, n)] + around
        )
        return jnp.where(m_ref[x + mx, pl.ds(y0 + my, n)] > 0.0, new, 0.0)

    def sweep_a(x):
        new = sweep(c, cp, x, 1, 10)
        a[x, pl.ds(1, 10)] = new
        ap[x, pl.ds(1, 10)] = up(new)

    loop(1, 11, sweep_a)

    def sweep_b(x):
        out[x - 2] = sweep(a, ap, x, 2, 8)

    loop(2, 10, sweep_b)


def kernel(
    loads, density, out, held_loads, held_density, block, e0, zsend, zrecv, g0, m0, d0, i0, v0, vp0, u0, up0, r0,
    t1, tm1, e1, u1x, g1, m1, d1, i1, v1, vp1, u1, up1, r1,
    t2, tm2, yz, x2, g2, m2, d2, i2, v2, vp2, u2, up2, r2,
    t3, tm3, g3, m3, d3, i3, v3, vp3, u3, up3,
    zs, c, cp, a, ap, f2, f1, f0,
    sin, s0, q0, s1, q1, s1u, q1u, sy, qy, sx, qx,
):
    gx, gy, gz = (lax.axis_index(axis) for axis in ("gx", "gy", "gz"))

    inputs = [
        pltpu.make_async_copy(loads, held_loads, sin.at[0]),
        pltpu.make_async_copy(density, held_density, sin.at[1]),
    ]
    for copy in inputs:
        copy.start()

    partners = {(dx, dy, dz) for dx in (-1, 0, 1) for dy in (-1, 0, 1) for dz in (-1, 0, 1)}
    partners |= {(0, dy, dz) for dy, dz in YZ23} | {(dx, 0, 0) for dx in RING}
    partners = sorted(partners - {(0, 0, 0)})
    barrier = pltpu.get_barrier_semaphore()
    for o in partners:
        pl.semaphore_signal(barrier, inc=1, device_id=device(*o), device_id_type=MESH)

    for copy in inputs:
        copy.wait()
    field = rows((8,) + TILE) % 4
    four = [held_loads[0], held_loads[1], held_loads[2], held_density[...]]
    for y in range(4):
        pair = turn_rows(four[3], (3 - y) % 8) if y != 3 else four[3]
        for f in range(3):
            pair = jnp.where(field == f, turn_rows(four[f], (f - y) % 8) if f != y else four[f], pair)
        block[:, y] = pair
        e0[pl.ds(4, 8), y + 4] = pair[:, 0:4]
        e0[pl.ds(4, 8), y + 8] = pair[:, 4:8]
    pl.semaphore_wait(barrier, len(partners))

    span = {-1: (4, 12, 3), 0: (4, 4, 8), 1: (8, 0, 4)}
    sent = []
    copies = []
    for n, (dx, dy) in enumerate(XY8):
        (ax, bx, cx), (ay, by, cy) = span[dx], span[dy]
        copies.append(
            pltpu.make_async_remote_copy(
                src_ref=e0.at[pl.ds(ax, cx), pl.ds(ay, cy)],
                dst_ref=e0.at[pl.ds(bx, cx), pl.ds(by, cy)],
                send_sem=s0.at[n], recv_sem=q0.at[n],
                device_id=device(dx, dy, 0), device_id_type=MESH,
            )
        )
        copies[-1].start()
    k16 = lax.broadcasted_iota(jnp.int32, (16, 128), 0)
    l16 = lax.broadcasted_iota(jnp.int32, (16, 128), 1)
    pick_low = jnp.where((l16 == 128 - ZHALO + k16) & (k16 < ZHALO), 1.0, 0.0).astype(F32)
    pick_high = jnp.where((l16 == k16) & (k16 < ZHALO), 1.0, 0.0).astype(F32)
    n = 8
    for dz, pick in ((-1, pick_high), (1, pick_low)):
        side = 0 if dz > 0 else 1
        for half in (0, 1):
            zsend[side, half] = lax.dot_general(
                pick, block[pl.ds(half * 4, 4)].reshape(128, 128), (((1,), (1,)), ((), ())),
                precision=lax.Precision.HIGHEST, preferred_element_type=F32,
            )
        for dx, dy in itertools.product((-1, 0, 1), repeat=2):
            first, count = {-1: (0, 1), 0: (0, 2), 1: (1, 1)}[dx]
            copies.append(
                pltpu.make_async_remote_copy(
                    src_ref=zsend.at[side, pl.ds(first, count)],
                    dst_ref=zrecv.at[side, 1 - dx, 1 - dy, pl.ds(first, count)],
                    send_sem=s0.at[n], recv_sem=q0.at[n],
                    device_id=device(dx, dy, dz), device_id_type=MESH,
                )
            )
            copies[-1].start()
            n += 1

    def rim2(x):
        m2[x] = jnp.zeros((28,) + TILE, F32)

    loop(0, 28, rim2)
    for ref in (v2, vp2, u2, up2, r2):
        for j in (5, 22):
            ref[j, pl.ds(5, 18)] = jnp.zeros((18,) + TILE, F32)
            ref[pl.ds(5, 18), j] = jnp.zeros((18,) + TILE, F32)

    def rim3(x):
        for ref in (m3, v3, vp3, u3, up3):
            ref[x] = jnp.zeros((16,) + TILE, F32)

    loop(0, 16, rim3)
    for copy in copies:
        copy.wait_recv()
    sent += copies

    low_in, high_in = jnp.where(gz > 0, 1.0, 0.0), jnp.where(gz < SIDE - 1, 1.0, 0.0)
    put = jnp.concatenate([pick_low, pick_high], axis=0)
    for rx, ry in itertools.product((-1, 0, 1), repeat=2):
        inside = None
        if rx:
            inside = gx > 0 if rx < 0 else gx < SIDE - 1
        if ry:
            more = gy > 0 if ry < 0 else gy < SIDE - 1
            inside = more if inside is None else inside & more
        factor = 1.0 if inside is None else jnp.where(inside, 1.0, 0.0)
        for half in {-1: (1,), 0: (0, 1), 1: (0,)}[rx]:
            both = jnp.concatenate([zrecv[0, rx + 1, ry + 1, half], zrecv[1, rx + 1, ry + 1, half]], axis=0)
            ends = lax.dot_general(
                both, put, (((0,), (0,)), ((), ())),
                precision=lax.Precision.HIGHEST, preferred_element_type=F32,
            ).reshape((4, 4) + TILE)
            x_at, nx = 4 + 8 * rx + 4 * half, 3 if rx > 0 else 4
            for late in {-1: (1,), 0: (0, 1), 1: (0,)}[ry]:
                y_at, ny = 4 + 8 * ry + 4 * late, 3 if ry > 0 else 4
                shape = (nx, ny) + TILE
                spot = (pl.ds(x_at, nx), pl.ds(y_at, ny))
                top, lane = rows(shape) < 4, lanes(shape)
                held = ends[0:nx, 0:ny]
                if not late:
                    held = turn_rows(held, 4)
                whole = jnp.where(top, twice(e0[spot]), held)
                dens = jnp.where(top, spread(whole, 3), spread(whole, 7))
                ok = jnp.where(
                    top, 1.0,
                    jnp.where(lane < ZHALO, high_in, jnp.where(lane >= 128 - ZHALO, low_in, 0.0)),
                ) * factor
                g0[spot] = (1.8 * ok) * whole
                m0[spot] = (0.15 * ok) * (0.001 + (1.0 - 0.001) * (dens * dens * dens))

    diagonal(m0, d0, i0, g0, v0, vp0, (1, 15), (1, 14), up_pair, down_pair)
    smooth(v0, vp0, m0, i0, g0, u0, up0, (2, 14), (2, 12), up_pair, down_pair)
    residual(u0, up0, m0, d0, g0, r0, (3, 12), (3, 9), down_pair)
    restrict_xy(r0, t1, 4, 4)
    coarsen_xy(m0, tm1, 4, 4)
    top128 = rows((16,) + TILE) < 4

    def both_ends(tiles, kind):
        flat = tiles[...].reshape(128, 128)
        parts = [product(flat, kind(where)).reshape((16,) + TILE) for where in ("all", "beyond")]
        joined = jnp.where(top128, parts[0], parts[1])
        return joined + turn_rows(joined, 4)

    new_g, new_m = both_ends(t1, restriction), both_ends(tm1, coarsening)
    joined = jnp.where(rows((16,) + TILE) == 3, new_m, new_g)[:, 0:4]
    e1[pl.ds(4, 4), pl.ds(4, 4)] = joined.reshape(4, 4, 4, 128)

    def blocks8(ref, send, recv):
        found = []
        for n, (dx, dy) in enumerate(XY8):
            found.append(
                pltpu.make_async_remote_copy(
                    src_ref=ref.at[pl.ds(4, 4), pl.ds(4, 4)],
                    dst_ref=ref.at[pl.ds({-1: 8, 0: 4, 1: 0}[dx], 4), pl.ds({-1: 8, 0: 4, 1: 0}[dy], 4)],
                    send_sem=send.at[n], recv_sem=recv.at[n],
                    device_id=device(dx, dy, 0), device_id_type=MESH,
                )
            )
        return found

    copies = blocks8(e1, s1, q1)
    for copy in copies:
        copy.start()
    for copy in copies:
        copy.wait_recv()
    sent += copies

    y_index = lax.broadcasted_iota(jnp.int32, (12,) + TILE, 0)
    inside_y = jnp.where(y_index < 4, jnp.where(gy > 0, 1.0, 0.0), jnp.where(y_index < 8, 1.0, jnp.where(gy < SIDE - 1, 1.0, 0.0)))

    def take1(x):
        inside_x = jnp.where(((x >= 4) | (gx > 0)) & ((x < 8) | (gx < SIDE - 1)), 1.0, 0.0)
        whole = twice(e1[x]) * (inside_x * inside_y)
        mod = spread(whole, 3)
        m1[x] = mod
        g1[x] = jnp.where(mod > 0.0, whole, 0.0)

    loop(0, 12, take1)
    diagonal(m1, d1, i1, g1, v1, vp1, (1, 12), (1, 11), up_plain, down_plain)
    smooth(v1, vp1, m1, i1, g1, u1, up1, (2, 9), (2, 7), up_plain, down_plain)
    own = (pl.ds(4, 4), pl.ds(4, 4))
    u1x[own] = u1[own][:, :, 0:4]
    u_copies = blocks8(u1x, s1u, q1u)
    residual(u1, up1, m1, d1, g1, r1, (3, 8), (3, 5), down_plain)
    restrict_xy(r1, t2, 4, 2)
    coarsen_xy(m1, tm2, 4, 2)
    new_g = product(t2[...].reshape(32, 128), restriction("round"))
    new_m = product(tm2[...].reshape(32, 128), coarsening("round"))
    both = jnp.where(rows((32, 128)) % 8 == 3, new_m, new_g)
    both = jnp.where(lanes((32, 128)) < 32, both, 0.0).reshape((2, 2) + TILE)
    yz[1, :, pl.ds(2 * gy, 2)] = both[:, :, 0:4]

    copies = []
    for n, (dy, dz) in enumerate(YZ23):
        copies.append(
            pltpu.make_async_remote_copy(
                src_ref=yz.at[1, :, pl.ds(2 * gy, 2)],
                dst_ref=yz.at[1 - dz, :, pl.ds(2 * gy, 2)],
                send_sem=sy.at[n], recv_sem=qy.at[n],
                device_id=device(0, dy, dz), device_id_type=MESH,
            )
        )
    for copy in copies + u_copies:
        copy.start()
    for copy in copies:
        copy.wait_recv()
    sent += copies + u_copies
    x2[pl.ds(2 * gx, 2)] = (
        yz[1] + turn_lanes(yz[0], 96) * low_in + turn_lanes(yz[2], 32) * high_in
    )

    copies = []
    for n, dx in enumerate(RING):
        copies.append(
            pltpu.make_async_remote_copy(
                src_ref=x2.at[pl.ds(2 * gx, 2)],
                dst_ref=x2.at[pl.ds(2 * gx, 2)],
                send_sem=sx.at[n], recv_sem=qx.at[n],
                device_id=device(dx, 0, 0), device_id_type=MESH,
            )
        )
    for copy in copies:
        copy.start()
    for copy in copies:
        copy.wait_recv()
    sent += copies

    def take2(x):
        whole = twice(x2[x])
        mod = spread(whole, 3)
        m2[x + 6, pl.ds(6, 16)] = mod
        g2[x + 6, pl.ds(6, 16)] = jnp.where(mod > 0.0, whole, 0.0)

    loop(0, 16, take2)
    diagonal(m2, d2, i2, g2, v2, vp2, (6, 22), (6, 16), up_plain, down_plain)
    smooth(v2, vp2, m2, i2, g2, u2, up2, (6, 22), (6, 16), up_plain, down_plain)
    residual(u2, up2, m2, d2, g2, r2, (6, 22), (6, 16), down_plain)
    restrict_xy(r2, t3, 6, 8)
    coarsen_xy(m2, tm3, 6, 8)
    new_g = product(t3[...].reshape(512, 128), restriction("round")).reshape(8, 8, 8, 128)
    new_m = product(tm3[...].reshape(512, 128), coarsening("round")).reshape(8, 8, 8, 128)
    m3[pl.ds(4, 8), pl.ds(4, 8)] = new_m
    g3[pl.ds(4, 8), pl.ds(4, 8)] = jnp.where(new_m > 0.0, new_g, 0.0)

    diagonal(m3, d3, i3, g3, v3, vp3, (4, 12), (4, 8), up_plain, down_plain)

    def two(i):
        smooth(v3, vp3, m3, i3, g3, u3, up3, (4, 12), (4, 8), up_plain, down_plain)
        smooth(u3, up3, m3, i3, g3, v3, vp3, (4, 12), (4, 8), up_plain, down_plain)

    loop(0, 3, two)
    smooth(v3, vp3, m3, i3, g3, u3, up3, (4, 12), (4, 8), up_plain, down_plain)

    x_at, y_at = 2 * gx + 2, 2 * gy + 2
    rise(
        u3[pl.ds(gx + 2, 7), pl.ds(gy + 2, 7)],
        (prolongation("round"),),
        lambda x: u2[x + x_at, pl.ds(y_at, 12)],
        (m2, x_at, y_at), (i2, x_at, y_at), (g2, x_at, y_at),
        zs, c, cp, a, ap, f2, up_plain, down_plain,
    )
    for copy in u_copies:
        copy.wait_recv()
    rise(
        f2[pl.ds(0, 7), pl.ds(0, 7)],
        (prolongation("round"),),
        lambda x: twice(u1x[x]),
        (m1, 0, 0), (i1, 0, 0), (g1, 0, 0),
        zs, c, cp, a, ap, f1, up_plain, down_plain,
    )

    rise(
        f1[pl.ds(1, 7), pl.ds(1, 7)],
        (prolongation("all"), prolongation("beyond")),
        lambda x: u0[x + 2, pl.ds(2, 12)],
        (m0, 2, 2), (i0, 2, 2), (g0, 2, 2),
        zs, c, cp, a, ap, f0, up_pair, down_pair,
    )
    for f in range(3):
        plane = f0[:, f]
        for y in range(8):
            if y != f:
                plane = jnp.where(rows((8,) + TILE) == y, turn_rows(f0[:, y], (y - f) % 8), plane)
        out[f] = plane
    for copy in sent:
        copy.wait_send()


def per_device(loads, density):
    def tiles(*lead):
        return pltpu.VMEM(lead + TILE, F32)

    def thin(*lead):
        return pltpu.VMEM(lead + (4, 128), F32)

    sems = [pltpu.SemaphoreType.DMA((2,))]
    for count in (26, 8, 8, 23, 7):
        sems += [pltpu.SemaphoreType.DMA((count,))] * 2
    return pl.pallas_call(
        kernel,
        out_shape=jax.ShapeDtypeStruct((3,) + (8,) + TILE, F32),
        in_specs=[pl.BlockSpec(memory_space=pl.ANY)] * 2,
        out_specs=pl.BlockSpec(memory_space=pltpu.VMEM),
        scratch_shapes=[tiles(3, 8), tiles(8), tiles(8, 4), thin(15, 15), pltpu.VMEM((2, 2, 16, 128), F32), pltpu.VMEM((2, 3, 3, 2, 16, 128), F32)]
        + [tiles(15, 15)] * 9
        + [tiles(4, 4)] * 2
        + [thin(12, 12)] * 2
        + [tiles(12, 12)] * 9
        + [tiles(2, 2)] * 2
        + [thin(3, 2, 16), thin(16, 16)]
        + [tiles(28, 28)] * 9
        + [tiles(8, 8)] * 2
        + [tiles(16, 16)] * 8
        + [tiles(7, 7)]
        + [tiles(12, 12)] * 4
        + [tiles(8, 8)] * 3
        + sems,
        compiler_params=pltpu.CompilerParams(
            collective_id=0, has_side_effects=True, vmem_limit_bytes=60 * 2**20
        ),
        cost_estimate=pl.CostEstimate(flops=10**8, bytes_accessed=10**6, transcendentals=0),
    )(loads, density)


def solution(mesh):
    placed = (P(None, "gx", "gy", "gz"), P("gx", "gy", "gz"))
    return jax.shard_map(
        per_device, mesh=mesh, in_specs=placed, out_specs=P(None, "gx", "gy", "gz"), check_vma=False
    )
```

time: 90.5 us -> 66.5 us (0.73)
  Pallas kernels: 87 us -> 64.8 us
  other arithmetic: 0.92 us -> 0 us
    pallas_call x1, Pallas kernels: 87 us -> 64.8 us  [per_device(): pl.pallas_call(kernel, out_shape=jax.ShapeDtypeStruct((3,) + (8,) + TILE,...]
    slice x1 -> x0, local copies, waits for them, and re-layouts: 0.97 us -> none  [per_device(): return jnp.transpose(result.reshape(8, 8, 8, 128)[:, :, :3], (2, 0, 1, 3))]
    concatenate x1 -> x0, other arithmetic: 0.92 us -> none  [per_device(): jnp.concatenate([jnp.transpose(loads, (1, 2, 0, 3)), density[:, :, None]]...]
where the time goes in v2:
time: 66.5 us; the launch traced here: 66.3 us
  Pallas kernels  64.8 us (97%)
  local copies, waits for them, and re-layouts  1.54 us (2%)
    pallas_call x1, Pallas kernels, per_device(): pl.pallas_call(kernel, out_shape=jax.ShapeDtypeStruct((3,) + (8,) + TILE,...  64.8 us
    unnamed x1, local copies, waits for them, and re-layouts  1.54 us

profile of v2, /device:TPU:1, one launch (start us, length us, event | category | flops | bytes accessed | tf_op | source)
XLA Modules:
  0.0 66.3 jit_solution(6176423540279971969)
XLA Ops:
  0.0 64.8 %shard_map.28 = f32[3,8,8,128]{3,2,1,0:T(8,128)} custom-call(f32[3,8,8,128]{3,2,1,0:T(8,128)} %loads.1, f32[8,8,128]{2,1,0:T(8,128)} %density.1), custom_call_target="tpu_custom_call" | custom-call | flops 100000000 | bytes 1000000 | tf_op jit(solution)/shard_map/pallas_call | solution.py:540
  64.8 1.5 %copy.4 = f32[3,8,8,128]{3,2,1,0:T(8,128)} copy(f32[3,8,8,128]{3,2,1,0:T(8,128)} %shard_map.28) | data formatting | bytes 196608

commit v3 on v2

--- a/solution.py
+++ b/solution.py
@@ -66,6 +66,17 @@
 
 def spread(tiles, row):
     return jnp.broadcast_to(tiles[..., row : row + 1, :], tiles.shape)
+
+
+def halves(tiles):
+    top, turned = rows(tiles.shape) < 4, turn_rows(tiles, 4)
+    return jnp.where(top, tiles, turned), jnp.where(top, turned, tiles)
+
+
+def put_rims(ref, x, line):
+    top, n = rows() < 4, line.shape[0]
+    ref[x, 0] = jnp.where(top, 0.0, turn_rows(line[n - 1], 4))
+    ref[x, n + 1] = jnp.where(top, turn_rows(line[0], 4), 0.0)
 
 
 def stencil(v, vp, m, ix, y0, n, mx, my, down):
@@ -101,7 +112,15 @@
         lax.fori_loop(0, count // each, step, 0)
 
 
-def diagonal(m, d4, inv, g, v, vp, xs, ys, up, down):
+def loop_rolled(lower, upper, body):
+    def step(i, carry):
+        body(i)
+        return carry
+
+    lax.fori_loop(lower, upper, step, 0)
+
+
+def diagonal(m, d4, inv, g, v, vp, xs, ys, up, down, rims=False, also=None):
     y0, n = ys
     at = pl.ds(y0, n)
 
@@ -113,37 +132,52 @@
         d4[x, at] = 4.0 * total
         inv[x, at] = share
         first = share * g[x, at]
+        above = up(first)
         v[x, at] = first
-        vp[x, at] = up(first)
+        vp[x, at] = above
+        if rims:
+            put_rims(v, x, first)
+            put_rims(vp, x, above)
+        if also is not None:
+            also(x, share)
 
     loop(xs[0], xs[1], body)
 
 
-def smooth(v, vp, m, inv, g, out, outp, xs, ys, up, down):
+def smooth(v, vp, m, inv, g, out, outp, xs, ys, up, down, rims=False, also=None):
     y0, n = ys
     at = pl.ds(y0, n)
 
     def body(x):
         around = stencil(v, vp, m, x, y0, n, x, 0, down)
         new = 0.4 * v[x, at] + inv[x, at] * (g[x, at] + around)
+        above = up(new)
         out[x, at] = new
-        outp[x, at] = up(new)
+        outp[x, at] = above
+        if rims:
+            put_rims(out, x, new)
+            put_rims(outp, x, above)
+        if also is not None:
+            also(x, new)
 
     loop(xs[0], xs[1], body)
 
 
-def residual(v, vp, m, d4, g, out, xs, ys, down):
+def residual(v, vp, m, d4, g, out, xs, ys, down, rims=False):
     y0, n = ys
     at = pl.ds(y0, n)
 
     def body(x):
         around = stencil(v, vp, m, x, y0, n, x, 0, down)
-        out[x, at] = (g[x, at] - d4[x, at] * v[x, at]) + around
+        left = (g[x, at] - d4[x, at] * v[x, at]) + around
+        out[x, at] = left
+        if rims:
+            put_rims(out, x, left)
 
     loop(xs[0], xs[1], body)
 
 
-def restrict_xy(res, out, base, count):
+def restrict_xy(res, out, base, count_x, count):
     def body(i):
         x = base + 2 * i
         wide = pl.ds(base - 1, 2 * count + 1)
@@ -151,10 +185,10 @@
         for k in range(count):
             out[i, k] = line[2 * k + 1] + 0.5 * (line[2 * k] + line[2 * k + 2])
 
-    loop(0, count, body)
-
-
-def coarsen_xy(m, out, base, count):
+    loop(0, count_x, body)
+
+
+def coarsen_xy(m, out, base, count_x, count):
     def body(i):
         x = base + 2 * i
         wide = pl.ds(base, 2 * count)
@@ -162,7 +196,7 @@
         for k in range(count):
             out[i, k] = line[2 * k] + line[2 * k + 1]
 
-    loop(0, count, body)
+    loop(0, count_x, body)
 
 
 def place(index, own):
@@ -244,8 +278,8 @@
 def kernel(
     loads, density, out, held_loads, held_density, block, e0, zsend, zrecv, g0, m0, d0, i0, v0, vp0, u0, up0, r0,
     t1, tm1, e1, u1x, g1, m1, d1, i1, v1, vp1, u1, up1, r1,
-    t2, tm2, yz, x2, g2, m2, d2, i2, v2, vp2, u2, up2, r2,
-    t3, tm3, g3, m3, d3, i3, v3, vp3, u3, up3,
+    t2, tm2, yz, x2, g2, m2, i2, u2, g2h, m2h, d2, i2h, v2, vp2, u2h, up2, r2,
+    t3, tm3, u3, g3, m3, d3, i3, v3, vp3, u3h, up3,
     zs, c, cp, a, ap, f2, f1, f0,
     sin, s0, q0, s1, q1, s1u, q1u, sy, qy, sx, qx,
 ):
@@ -321,14 +355,19 @@
         m2[x] = jnp.zeros((28,) + TILE, F32)
 
     loop(0, 28, rim2)
-    for ref in (v2, vp2, u2, up2, r2):
-        for j in (5, 22):
-            ref[j, pl.ds(5, 18)] = jnp.zeros((18,) + TILE, F32)
-            ref[pl.ds(5, 18), j] = jnp.zeros((18,) + TILE, F32)
+    line = jnp.zeros((10,) + TILE, F32)
+    for ref in (m2h, v2, vp2, u2h, up2, r2):
+        ref[0] = line
+    for ref in (v2, vp2, u2h, up2):
+        ref[17] = line
+    line = jnp.zeros((6,) + TILE, F32)
+    m3[0] = line
+    for ref in (v3, vp3, u3h, up3):
+        ref[0] = line
+        ref[9] = line
 
     def rim3(x):
-        for ref in (m3, v3, vp3, u3, up3):
-            ref[x] = jnp.zeros((16,) + TILE, F32)
+        u3[x] = jnp.zeros((16,) + TILE, F32)
 
     loop(0, 16, rim3)
     for copy in copies:
@@ -372,8 +411,8 @@
     diagonal(m0, d0, i0, g0, v0, vp0, (1, 15), (1, 14), up_pair, down_pair)
     smooth(v0, vp0, m0, i0, g0, u0, up0, (2, 14), (2, 12), up_pair, down_pair)
     residual(u0, up0, m0, d0, g0, r0, (3, 12), (3, 9), down_pair)
-    restrict_xy(r0, t1, 4, 4)
-    coarsen_xy(m0, tm1, 4, 4)
+    restrict_xy(r0, t1, 4, 4, 4)
+    coarsen_xy(m0, tm1, 4, 4, 4)
     top128 = rows((16,) + TILE) < 4
 
     def both_ends(tiles, kind):
@@ -423,32 +462,55 @@
     u1x[own] = u1[own][:, :, 0:4]
     u_copies = blocks8(u1x, s1u, q1u)
     residual(u1, up1, m1, d1, g1, r1, (3, 8), (3, 5), down_plain)
-    restrict_xy(r1, t2, 4, 2)
-    coarsen_xy(m1, tm2, 4, 2)
+    restrict_xy(r1, t2, 4, 2, 2)
+    coarsen_xy(m1, tm2, 4, 2, 2)
     new_g = product(t2[...].reshape(32, 128), restriction("round"))
     new_m = product(tm2[...].reshape(32, 128), coarsening("round"))
-    both = jnp.where(rows((32, 128)) % 8 == 3, new_m, new_g)
-    both = jnp.where(lanes((32, 128)) < 32, both, 0.0).reshape((2, 2) + TILE)
-    yz[1, :, pl.ds(2 * gy, 2)] = both[:, :, 0:4]
+    both = jnp.where(rows((32, 128)) % 8 == 3, new_m, new_g).reshape((4,) + TILE)
+    group = lanes((4,) + TILE) // 32
+    packed = jnp.where(group == 0, spread(both, 0), 0.0)
+    for f in (1, 2, 3):
+        packed = jnp.where(group == f, spread(turn_lanes(both, 32 * f), f), packed)
+    line = packed[0]
+    for k in (1, 2, 3):
+        line = jnp.where(rows() == k, packed[k], line)
+    yz[1, gy] = line[0:4]
 
     copies = []
     for n, (dy, dz) in enumerate(YZ23):
         copies.append(
             pltpu.make_async_remote_copy(
-                src_ref=yz.at[1, :, pl.ds(2 * gy, 2)],
-                dst_ref=yz.at[1 - dz, :, pl.ds(2 * gy, 2)],
+                src_ref=yz.at[1, gy],
+                dst_ref=yz.at[1 - dz, gy],
                 send_sem=sy.at[n], recv_sem=qy.at[n],
                 device_id=device(0, dy, dz), device_id_type=MESH,
             )
         )
-    for copy in copies + u_copies:
+    for copy in copies:
         copy.start()
     for copy in copies:
         copy.wait_recv()
-    sent += copies + u_copies
-    x2[pl.ds(2 * gx, 2)] = (
-        yz[1] + turn_lanes(yz[0], 96) * low_in + turn_lanes(yz[2], 32) * high_in
-    )
+    sent += copies
+    shape = (8,) + TILE
+    group, field = lanes(shape) // 32, rows(shape) % 4
+    is_own = group == field
+    is_high, is_low = group == (field + 1) % 4, group == (field + 3) % 4
+    low = twice(turn_lanes(yz[0], 96) * low_in)
+    own = twice(yz[1])
+    high = twice(turn_lanes(yz[2], 32) * high_in)
+    columns = []
+    for k in range(4):
+        whole = jnp.where(is_high, spread(high, k), 0.0)
+        whole = jnp.where(is_low, spread(low, k), whole)
+        whole = jnp.where(is_own, spread(own, k), whole)
+        turned = [whole] + [turn_lanes(whole, 128 - 32 * f) for f in (1, 2, 3)]
+        for f in (1, 2, 3):
+            whole = jnp.where(field == f, turned[f], whole)
+        columns.append(whole)
+    for x in range(2):
+        for y in range(8):
+            x2[2 * gx + x, 2 * y] = columns[2 * x][y, 0:4]
+            x2[2 * gx + x, 2 * y + 1] = columns[2 * x + 1][y, 0:4]
 
     copies = []
     for n, dx in enumerate(RING):
@@ -466,31 +528,59 @@
         copy.wait_recv()
     sent += copies
 
+    for copy in u_copies:
+        copy.start()
+    sent += u_copies
+
     def take2(x):
         whole = twice(x2[x])
         mod = spread(whole, 3)
         m2[x + 6, pl.ds(6, 16)] = mod
         g2[x + 6, pl.ds(6, 16)] = jnp.where(mod > 0.0, whole, 0.0)
+        whole = jnp.concatenate([x2[x, pl.ds(0, 8)], x2[x, pl.ds(8, 8)]], axis=1)
+        mod = jnp.where(rows((8,) + TILE) < 4, spread(whole, 3), spread(whole, 7))
+        m2h[x + 1, pl.ds(1, 8)] = mod
+        put_rims(m2h, x + 1, mod)
+        g2h[x + 1, pl.ds(1, 8)] = jnp.where(mod > 0.0, whole, 0.0)
 
     loop(0, 16, take2)
-    diagonal(m2, d2, i2, g2, v2, vp2, (6, 22), (6, 16), up_plain, down_plain)
-    smooth(v2, vp2, m2, i2, g2, u2, up2, (6, 22), (6, 16), up_plain, down_plain)
-    residual(u2, up2, m2, d2, g2, r2, (6, 22), (6, 16), down_plain)
-    restrict_xy(r2, t3, 6, 8)
-    coarsen_xy(m2, tm3, 6, 8)
-    new_g = product(t3[...].reshape(512, 128), restriction("round")).reshape(8, 8, 8, 128)
-    new_m = product(tm3[...].reshape(512, 128), coarsening("round")).reshape(8, 8, 8, 128)
-    m3[pl.ds(4, 8), pl.ds(4, 8)] = new_m
-    g3[pl.ds(4, 8), pl.ds(4, 8)] = jnp.where(new_m > 0.0, new_g, 0.0)
-
-    diagonal(m3, d3, i3, g3, v3, vp3, (4, 12), (4, 8), up_plain, down_plain)
+
+    def whole2(ref):
+        def store(x, line):
+            first, second = halves(line)
+            ref[x + 5, pl.ds(6, 8)] = first
+            ref[x + 5, pl.ds(14, 8)] = second
+
+        return store
+
+    span = ((1, 17), (1, 8), up_plain, down_plain, True)
+    diagonal(m2h, d2, i2h, g2h, v2, vp2, *span, whole2(i2))
+    smooth(v2, vp2, m2h, i2h, g2h, u2h, up2, *span, whole2(u2))
+    residual(u2h, up2, m2h, d2, g2h, r2, (1, 17), (1, 8), down_plain, True)
+    restrict_xy(r2, t3, 1, 8, 4)
+    coarsen_xy(m2h, tm3, 1, 8, 4)
+    new_g = product(t3[...].reshape(256, 128), restriction("round")).reshape(8, 4, 8, 128)
+    new_m = product(tm3[...].reshape(256, 128), coarsening("round")).reshape(8, 4, 8, 128)
+    for x in range(8):
+        m3[x + 1, pl.ds(1, 4)] = new_m[x]
+        put_rims(m3, x + 1, new_m[x])
+        g3[x + 1, pl.ds(1, 4)] = jnp.where(new_m[x] > 0.0, new_g[x], 0.0)
+
+    span = ((1, 9), (1, 4), up_plain, down_plain, True)
+    diagonal(m3, d3, i3, g3, v3, vp3, *span)
 
     def two(i):
-        smooth(v3, vp3, m3, i3, g3, u3, up3, (4, 12), (4, 8), up_plain, down_plain)
-        smooth(u3, up3, m3, i3, g3, v3, vp3, (4, 12), (4, 8), up_plain, down_plain)
-
-    loop(0, 3, two)
-    smooth(v3, vp3, m3, i3, g3, u3, up3, (4, 12), (4, 8), up_plain, down_plain)
+        smooth(v3, vp3, m3, i3, g3, u3h, up3, *span)
+        smooth(u3h, up3, m3, i3, g3, v3, vp3, *span)
+
+    loop_rolled(0, 3, two)
+
+    def whole3(x, line):
+        first, second = halves(line)
+        u3[x + 3, pl.ds(4, 4)] = first
+        u3[x + 3, pl.ds(8, 4)] = second
+
+    smooth(v3, vp3, m3, i3, g3, u3h, up3, *span, whole3)
 
     x_at, y_at = 2 * gx + 2, 2 * gy + 2
     rise(
@@ -548,10 +638,12 @@
         + [thin(12, 12)] * 2
         + [tiles(12, 12)] * 9
         + [tiles(2, 2)] * 2
-        + [thin(3, 2, 16), thin(16, 16)]
-        + [tiles(28, 28)] * 9
-        + [tiles(8, 8)] * 2
-        + [tiles(16, 16)] * 8
+        + [thin(3, 8), thin(16, 16)]
+        + [tiles(28, 28)] * 4
+        + [tiles(18, 10)] * 9
+        + [tiles(8, 4)] * 2
+        + [tiles(16, 16)]
+        + [tiles(10, 6)] * 8
         + [tiles(7, 7)]
         + [tiles(12, 12)] * 4
         + [tiles(8, 8)] * 3

time: 66.5 us -> 62 us (0.932)
  Pallas kernels: 64.8 us -> 60.3 us
    pallas_call x1, Pallas kernels: 64.8 us -> 60.3 us  [per_device(): pl.pallas_call(kernel, out_shape=jax.ShapeDtypeStruct((3,) + (8,) + TILE,...]
where the time goes in v3:
time: 62 us; the launch traced here: 61.8 us
  Pallas kernels  60.3 us (97%)
  local copies, waits for them, and re-layouts  1.54 us (2%)
    pallas_call x1, Pallas kernels, per_device(): pl.pallas_call(kernel, out_shape=jax.ShapeDtypeStruct((3,) + (8,) + TILE,...  60.3 us
    unnamed x1, local copies, waits for them, and re-layouts  1.54 us

profile of v3, /device:TPU:1, one launch (start us, length us, event | category | flops | bytes accessed | tf_op | source)
XLA Modules:
  0.0 61.8 jit_solution(934420650706309494)
XLA Ops:
  0.0 60.3 %shard_map.28 = f32[3,8,8,128]{3,2,1,0:T(8,128)} custom-call(f32[3,8,8,128]{3,2,1,0:T(8,128)} %loads.1, f32[8,8,128]{2,1,0:T(8,128)} %density.1), custom_call_target="tpu_custom_call" | custom-call | flops 100000000 | bytes 1000000 | tf_op jit(solution)/shard_map/pallas_call | solution.py:630
  60.3 1.5 %copy.4 = f32[3,8,8,128]{3,2,1,0:T(8,128)} copy(f32[3,8,8,128]{3,2,1,0:T(8,128)} %shard_map.28) | data formatting | bytes 196608

commit v4 on v3

--- a/solution.py
+++ b/solution.py
@@ -12,18 +12,24 @@
 F32 = jnp.float32
 TILE = (8, 128)
 SIDE = 8
-UNROLL = 8
+UNROLL = 16
 ZHALO = 12
 RING = (1, 2, 3, 4, -3, -2, -1)
 XY8 = [(dx, dy) for dx in (-1, 0, 1) for dy in (-1, 0, 1) if dx or dy]
 YZ23 = [(dy, dz) for dy in (0,) + RING for dz in (-1, 0, 1) if dy or dz]
 
 
-def device(dx, dy, dz):
-    return tuple(
-        lax.rem(lax.axis_index(axis) + (step + SIDE), SIDE)
-        for axis, step in (("gx", dx), ("gy", dy), ("gz", dz))
-    )
+def around():
+    here = [lax.axis_index(axis) for axis in ("gx", "gy", "gz")]
+    known = [{0: at} for at in here]
+
+    def device(*steps):
+        for at, seen, step in zip(here, known, steps):
+            if step % SIDE not in seen:
+                seen[step % SIDE] = lax.rem(at + step % SIDE, SIDE)
+        return tuple(seen[step % SIDE] for seen, step in zip(known, steps))
+
+    return device
 
 
 def lanes(shape=TILE):
@@ -283,7 +289,8 @@
     zs, c, cp, a, ap, f2, f1, f0,
     sin, s0, q0, s1, q1, s1u, q1u, sy, qy, sx, qx,
 ):
-    gx, gy, gz = (lax.axis_index(axis) for axis in ("gx", "gy", "gz"))
+    device = around()
+    gx, gy, gz = device(0, 0, 0)
 
     inputs = [
         pltpu.make_async_copy(loads, held_loads, sin.at[0]),
@@ -291,6 +298,8 @@
     ]
     for copy in inputs:
         copy.start()
+    for step in RING:
+        device(step, step, step)
 
     partners = {(dx, dy, dz) for dx in (-1, 0, 1) for dy in (-1, 0, 1) for dz in (-1, 0, 1)}
     partners |= {(0, dy, dz) for dy, dz in YZ23} | {(dx, 0, 0) for dx in RING}
@@ -310,6 +319,16 @@
         block[:, y] = pair
         e0[pl.ds(4, 8), y + 4] = pair[:, 0:4]
         e0[pl.ds(4, 8), y + 8] = pair[:, 4:8]
+    k16 = lax.broadcasted_iota(jnp.int32, (16, 128), 0)
+    l16 = lax.broadcasted_iota(jnp.int32, (16, 128), 1)
+    pick_low = jnp.where((l16 == 128 - ZHALO + k16) & (k16 < ZHALO), 1.0, 0.0).astype(F32)
+    pick_high = jnp.where((l16 == k16) & (k16 < ZHALO), 1.0, 0.0).astype(F32)
+    for side, pick in enumerate((pick_low, pick_high)):
+        for half in (0, 1):
+            zsend[side, half] = lax.dot_general(
+                pick, block[pl.ds(half * 4, 4)].reshape(128, 128), (((1,), (1,)), ((), ())),
+                precision=lax.Precision.HIGHEST, preferred_element_type=F32,
+            )
     pl.semaphore_wait(barrier, len(partners))
 
     span = {-1: (4, 12, 3), 0: (4, 4, 8), 1: (8, 0, 4)}
@@ -326,18 +345,9 @@
             )
         )
         copies[-1].start()
-    k16 = lax.broadcasted_iota(jnp.int32, (16, 128), 0)
-    l16 = lax.broadcasted_iota(jnp.int32, (16, 128), 1)
-    pick_low = jnp.where((l16 == 128 - ZHALO + k16) & (k16 < ZHALO), 1.0, 0.0).astype(F32)
-    pick_high = jnp.where((l16 == k16) & (k16 < ZHALO), 1.0, 0.0).astype(F32)
     n = 8
-    for dz, pick in ((-1, pick_high), (1, pick_low)):
+    for dz in (-1, 1):
         side = 0 if dz > 0 else 1
-        for half in (0, 1):
-            zsend[side, half] = lax.dot_general(
-                pick, block[pl.ds(half * 4, 4)].reshape(128, 128), (((1,), (1,)), ((), ())),
-                precision=lax.Precision.HIGHEST, preferred_element_type=F32,
-            )
         for dx, dy in itertools.product((-1, 0, 1), repeat=2):
             first, count = {-1: (0, 1), 0: (0, 2), 1: (1, 1)}[dx]
             copies.append(
@@ -376,7 +386,7 @@
 
     low_in, high_in = jnp.where(gz > 0, 1.0, 0.0), jnp.where(gz < SIDE - 1, 1.0, 0.0)
     put = jnp.concatenate([pick_low, pick_high], axis=0)
-    for rx, ry in itertools.product((-1, 0, 1), repeat=2):
+    for rx, ry in [(0, 0), (0, -1), (0, 1), (-1, 0), (1, 0), (-1, -1), (-1, 1), (1, -1), (1, 1)]:
         inside = None
         if rx:
             inside = gx > 0 if rx < 0 else gx < SIDE - 1

time: 62 us -> 57.1 us (0.921)
  Pallas kernels: 60.3 us -> 55.4 us
    pallas_call x1, Pallas kernels: 60.3 us -> 55.4 us  [per_device(): pl.pallas_call(kernel, out_shape=jax.ShapeDtypeStruct((3,) + (8,) + TILE,...]
where the time goes in v4:
time: 57.1 us; the launch traced here: 57 us
  Pallas kernels  55.4 us (97%)
  local copies, waits for them, and re-layouts  1.54 us (3%)
    pallas_call x1, Pallas kernels, per_device(): pl.pallas_call(kernel, out_shape=jax.ShapeDtypeStruct((3,) + (8,) + TILE,...  55.4 us
    unnamed x1, local copies, waits for them, and re-layouts  1.54 us

profile of v4, /device:TPU:1, one launch (start us, length us, event | category | flops | bytes accessed | tf_op | source)
XLA Modules:
  0.0 57.0 jit_solution(12789368547992352573)
XLA Ops:
  0.0 55.4 %shard_map.28 = f32[3,8,8,128]{3,2,1,0:T(8,128)} custom-call(f32[3,8,8,128]{3,2,1,0:T(8,128)} %loads.1, f32[8,8,128]{2,1,0:T(8,128)} %density.1), custom_call_target="tpu_custom_call" | custom-call | flops 100000000 | bytes 1000000 | tf_op jit(solution)/shard_map/pallas_call | solution.py:640
  55.4 1.5 %copy.4 = f32[3,8,8,128]{3,2,1,0:T(8,128)} copy(f32[3,8,8,128]{3,2,1,0:T(8,128)} %shard_map.28) | data formatting | bytes 196608

commit v5 on v4

--- a/solution.py
+++ b/solution.py
@@ -126,7 +126,7 @@
     lax.fori_loop(lower, upper, step, 0)
 
 
-def diagonal(m, d4, inv, g, v, vp, xs, ys, up, down, rims=False, also=None):
+def diagonal(m, d4, inv, xs, ys, down, also=None):
     y0, n = ys
     at = pl.ds(y0, n)
 
@@ -137,15 +137,24 @@
         share = jnp.where(m[x, at] > 0.0, 0.15 / total, 0.0)
         d4[x, at] = 4.0 * total
         inv[x, at] = share
-        first = share * g[x, at]
+        if also is not None:
+            also(x, share)
+
+    loop(xs[0], xs[1], body)
+
+
+def first_sweep(inv, g, v, vp, xs, ys, up, rims=False):
+    y0, n = ys
+    at = pl.ds(y0, n)
+
+    def body(x):
+        first = inv[x, at] * g[x, at]
         above = up(first)
         v[x, at] = first
         vp[x, at] = above
         if rims:
             put_rims(v, x, first)
             put_rims(vp, x, above)
-        if also is not None:
-            also(x, share)
 
     loop(xs[0], xs[1], body)
 
@@ -284,10 +293,10 @@
 def kernel(
     loads, density, out, held_loads, held_density, block, e0, zsend, zrecv, g0, m0, d0, i0, v0, vp0, u0, up0, r0,
     t1, tm1, e1, u1x, g1, m1, d1, i1, v1, vp1, u1, up1, r1,
-    t2, tm2, yz, x2, g2, m2, i2, u2, g2h, m2h, d2, i2h, v2, vp2, u2h, up2, r2,
+    t2, yz, yzm, xm, x2, g2, m2, i2, u2, g2h, m2h, d2, i2h, v2, vp2, u2h, up2, r2,
     t3, tm3, u3, g3, m3, d3, i3, v3, vp3, u3h, up3,
     zs, c, cp, a, ap, f2, f1, f0,
-    sin, s0, q0, s1, q1, s1u, q1u, sy, qy, sx, qx,
+    sin, s0, q0, s1, q1, s1u, q1u, sy, qy, sx, qx, sym, qym, sxm, qxm,
 ):
     device = around()
     gx, gy, gz = device(0, 0, 0)
@@ -418,7 +427,8 @@
                 g0[spot] = (1.8 * ok) * whole
                 m0[spot] = (0.15 * ok) * (0.001 + (1.0 - 0.001) * (dens * dens * dens))
 
-    diagonal(m0, d0, i0, g0, v0, vp0, (1, 15), (1, 14), up_pair, down_pair)
+    diagonal(m0, d0, i0, (1, 15), (1, 14), down_pair)
+    first_sweep(i0, g0, v0, vp0, (1, 15), (1, 14), up_pair)
     smooth(v0, vp0, m0, i0, g0, u0, up0, (2, 14), (2, 12), up_pair, down_pair)
     residual(u0, up0, m0, d0, g0, r0, (3, 12), (3, 9), down_pair)
     restrict_xy(r0, t1, 4, 4, 4)
@@ -451,6 +461,28 @@
     copies = blocks8(e1, s1, q1)
     for copy in copies:
         copy.start()
+
+    line = new_m.reshape((4, 4) + TILE)
+    line = line[:, 0] + line[:, 1], line[:, 2] + line[:, 3]
+    flat = jnp.stack([line[y][2 * x] + line[y][2 * x + 1] for x in (0, 1) for y in (0, 1)], axis=0)
+    flat = product(flat.reshape(32, 128), coarsening("round")).reshape((4,) + TILE)
+    line = flat[0]
+    for k in (1, 2, 3):
+        line = jnp.where(rows() == k, flat[k], line)
+    yzm[1, gy] = jnp.where(lanes() < 32, line, 0.0)[0:4]
+    m_copies = []
+    for n, (dy, dz) in enumerate(YZ23):
+        m_copies.append(
+            pltpu.make_async_remote_copy(
+                src_ref=yzm.at[1, gy],
+                dst_ref=yzm.at[1 - dz, gy],
+                send_sem=sym.at[n], recv_sem=qym.at[n],
+                device_id=device(0, dy, dz), device_id_type=MESH,
+            )
+        )
+    for copy in m_copies:
+        copy.start()
+    sent += m_copies
     for copy in copies:
         copy.wait_recv()
     sent += copies
@@ -466,20 +498,19 @@
         g1[x] = jnp.where(mod > 0.0, whole, 0.0)
 
     loop(0, 12, take1)
-    diagonal(m1, d1, i1, g1, v1, vp1, (1, 12), (1, 11), up_plain, down_plain)
+    diagonal(m1, d1, i1, (1, 12), (1, 11), down_plain)
+    first_sweep(i1, g1, v1, vp1, (1, 12), (1, 11), up_plain)
     smooth(v1, vp1, m1, i1, g1, u1, up1, (2, 9), (2, 7), up_plain, down_plain)
     own = (pl.ds(4, 4), pl.ds(4, 4))
     u1x[own] = u1[own][:, :, 0:4]
     u_copies = blocks8(u1x, s1u, q1u)
     residual(u1, up1, m1, d1, g1, r1, (3, 8), (3, 5), down_plain)
     restrict_xy(r1, t2, 4, 2, 2)
-    coarsen_xy(m1, tm2, 4, 2, 2)
     new_g = product(t2[...].reshape(32, 128), restriction("round"))
-    new_m = product(tm2[...].reshape(32, 128), coarsening("round"))
-    both = jnp.where(rows((32, 128)) % 8 == 3, new_m, new_g).reshape((4,) + TILE)
+    both = new_g.reshape((4,) + TILE)
     group = lanes((4,) + TILE) // 32
     packed = jnp.where(group == 0, spread(both, 0), 0.0)
-    for f in (1, 2, 3):
+    for f in (1, 2):
         packed = jnp.where(group == f, spread(turn_lanes(both, 32 * f), f), packed)
     line = packed[0]
     for k in (1, 2, 3):
@@ -498,9 +529,27 @@
         )
     for copy in copies:
         copy.start()
+    sent += copies
+
+    for copy in m_copies:
+        copy.wait_recv()
+    xm[gx] = yzm[1] + turn_lanes(yzm[0], 96) * low_in + turn_lanes(yzm[2], 32) * high_in
+    m_copies = []
+    for n, dx in enumerate(RING):
+        m_copies.append(
+            pltpu.make_async_remote_copy(
+                src_ref=xm.at[gx],
+                dst_ref=xm.at[gx],
+                send_sem=sxm.at[n], recv_sem=qxm.at[n],
+                device_id=device(dx, 0, 0), device_id_type=MESH,
+            )
+        )
+    for copy in m_copies:
+        copy.start()
+    sent += m_copies
+
     for copy in copies:
         copy.wait_recv()
-    sent += copies
     shape = (8,) + TILE
     group, field = lanes(shape) // 32, rows(shape) % 4
     is_own = group == field
@@ -513,14 +562,16 @@
         whole = jnp.where(is_high, spread(high, k), 0.0)
         whole = jnp.where(is_low, spread(low, k), whole)
         whole = jnp.where(is_own, spread(own, k), whole)
-        turned = [whole] + [turn_lanes(whole, 128 - 32 * f) for f in (1, 2, 3)]
-        for f in (1, 2, 3):
-            whole = jnp.where(field == f, turned[f], whole)
-        columns.append(whole)
+        second = turn_lanes(whole, 96)
+        third = spread(turn_lanes(whole, 64), 2)
+        here = lanes(shape)
+        line = jnp.where((here >= 54) & (here < 107), turn_lanes(third, 75), whole)
+        other = jnp.where((here >= 54) & (here < 76), turn_lanes(third, 22), second)
+        columns.append(jnp.where(field == 0, line, other))
     for x in range(2):
         for y in range(8):
-            x2[2 * gx + x, 2 * y] = columns[2 * x][y, 0:4]
-            x2[2 * gx + x, 2 * y + 1] = columns[2 * x + 1][y, 0:4]
+            x2[2 * gx + x, 2 * y] = columns[2 * x][y, 0:2]
+            x2[2 * gx + x, 2 * y + 1] = columns[2 * x + 1][y, 0:2]
 
     copies = []
     for n, dx in enumerate(RING):
@@ -534,26 +585,22 @@
         )
     for copy in copies:
         copy.start()
-    for copy in copies:
+    sent += copies
+
+    for copy in m_copies:
         copy.wait_recv()
-    sent += copies
-
-    for copy in u_copies:
-        copy.start()
-    sent += u_copies
-
-    def take2(x):
-        whole = twice(x2[x])
-        mod = spread(whole, 3)
-        m2[x + 6, pl.ds(6, 16)] = mod
-        g2[x + 6, pl.ds(6, 16)] = jnp.where(mod > 0.0, whole, 0.0)
-        whole = jnp.concatenate([x2[x, pl.ds(0, 8)], x2[x, pl.ds(8, 8)]], axis=1)
-        mod = jnp.where(rows((8,) + TILE) < 4, spread(whole, 3), spread(whole, 7))
-        m2h[x + 1, pl.ds(1, 8)] = mod
-        put_rims(m2h, x + 1, mod)
-        g2h[x + 1, pl.ds(1, 8)] = jnp.where(mod > 0.0, whole, 0.0)
-
-    loop(0, 16, take2)
+
+    def take_m(i):
+        tile = twice(xm[i])
+        for x in range(2):
+            pair = jnp.stack([spread(tile, 2 * x), spread(tile, 2 * x + 1)], axis=1)
+            mod = pair.reshape((16,) + TILE)
+            m2[2 * i + x + 6, pl.ds(6, 16)] = mod
+            mod = jnp.where(rows((8,) + TILE) < 4, mod[0:8], mod[8:16])
+            m2h[2 * i + x + 1, pl.ds(1, 8)] = mod
+            put_rims(m2h, 2 * i + x + 1, mod)
+
+    loop(0, 8, take_m)
 
     def whole2(ref):
         def store(x, line):
@@ -563,21 +610,46 @@
 
         return store
 
-    span = ((1, 17), (1, 8), up_plain, down_plain, True)
-    diagonal(m2h, d2, i2h, g2h, v2, vp2, *span, whole2(i2))
-    smooth(v2, vp2, m2h, i2h, g2h, u2h, up2, *span, whole2(u2))
-    residual(u2h, up2, m2h, d2, g2h, r2, (1, 17), (1, 8), down_plain, True)
-    restrict_xy(r2, t3, 1, 8, 4)
+    diagonal(m2h, d2, i2h, (1, 17), (1, 8), down_plain, whole2(i2))
     coarsen_xy(m2h, tm3, 1, 8, 4)
-    new_g = product(t3[...].reshape(256, 128), restriction("round")).reshape(8, 4, 8, 128)
     new_m = product(tm3[...].reshape(256, 128), coarsening("round")).reshape(8, 4, 8, 128)
     for x in range(8):
         m3[x + 1, pl.ds(1, 4)] = new_m[x]
         put_rims(m3, x + 1, new_m[x])
-        g3[x + 1, pl.ds(1, 4)] = jnp.where(new_m[x] > 0.0, new_g[x], 0.0)
+    diagonal(m3, d3, i3, (1, 9), (1, 4), down_plain)
+    for copy in copies:
+        copy.wait_recv()
+
+    for copy in u_copies:
+        copy.start()
+    sent += u_copies
+
+    def take2(x):
+        whole = twice(twice(x2[x]))
+        here = lanes(whole.shape)
+        third = jnp.where(
+            (here < 32) | (here >= 107),
+            turn_lanes(spread(whole, 0), 128 - 75),
+            turn_lanes(spread(whole, 1), 128 - 22),
+        )
+        whole = jnp.where(rows(whole.shape) % 4 == 2, third, whole)
+        whole = jnp.where(m2[x + 6, pl.ds(6, 16)] > 0.0, whole, 0.0)
+        g2[x + 6, pl.ds(6, 16)] = whole
+        g2h[x + 1, pl.ds(1, 8)] = jnp.where(rows((8,) + TILE) < 4, whole[0:8], whole[8:16])
+
+    loop(0, 16, take2)
+
+    span = ((1, 17), (1, 8), up_plain, down_plain, True)
+    first_sweep(i2h, g2h, v2, vp2, (1, 17), (1, 8), up_plain, True)
+    smooth(v2, vp2, m2h, i2h, g2h, u2h, up2, *span, whole2(u2))
+    residual(u2h, up2, m2h, d2, g2h, r2, (1, 17), (1, 8), down_plain, True)
+    restrict_xy(r2, t3, 1, 8, 4)
+    new_g = product(t3[...].reshape(256, 128), restriction("round")).reshape(8, 4, 8, 128)
+    for x in range(8):
+        g3[x + 1, pl.ds(1, 4)] = jnp.where(m3[x + 1, pl.ds(1, 4)] > 0.0, new_g[x], 0.0)
 
     span = ((1, 9), (1, 4), up_plain, down_plain, True)
-    diagonal(m3, d3, i3, g3, v3, vp3, *span)
+    first_sweep(i3, g3, v3, vp3, (1, 9), (1, 4), up_plain, True)
 
     def two(i):
         smooth(v3, vp3, m3, i3, g3, u3h, up3, *span)
@@ -635,7 +707,7 @@
         return pltpu.VMEM(lead + (4, 128), F32)
 
     sems = [pltpu.SemaphoreType.DMA((2,))]
-    for count in (26, 8, 8, 23, 7):
+    for count in (26, 8, 8, 23, 7, 23, 7):
         sems += [pltpu.SemaphoreType.DMA((count,))] * 2
     return pl.pallas_call(
         kernel,
@@ -647,8 +719,8 @@
         + [tiles(4, 4)] * 2
         + [thin(12, 12)] * 2
         + [tiles(12, 12)] * 9
-        + [tiles(2, 2)] * 2
-        + [thin(3, 8), thin(16, 16)]
+        + [tiles(2, 2)]
+        + [thin(3, 8), thin(3, 8), thin(8, 8), pltpu.VMEM((16, 16, 2, 128), F32)]
         + [tiles(28, 28)] * 4
         + [tiles(18, 10)] * 9
         + [tiles(8, 4)] * 2

time: 57.1 us -> 55.5 us (0.972)
  Pallas kernels: 55.4 us -> 53.8 us
    pallas_call x1, Pallas kernels: 55.4 us -> 53.8 us  [per_device(): pl.pallas_call(kernel, out_shape=jax.ShapeDtypeStruct((3,) + (8,) + TILE,...]
where the time goes in v5:
time: 55.5 us; the launch traced here: 55.4 us
  Pallas kernels  53.8 us (97%)
  local copies, waits for them, and re-layouts  1.54 us (3%)
    pallas_call x1, Pallas kernels, per_device(): pl.pallas_call(kernel, out_shape=jax.ShapeDtypeStruct((3,) + (8,) + TILE,...  53.8 us
    unnamed x1, local copies, waits for them, and re-layouts  1.54 us

profile of v5, /device:TPU:1, one launch (start us, length us, event | category | flops | bytes accessed | tf_op | source)
XLA Modules:
  0.0 55.4 jit_solution(13215537075011990443)
XLA Ops:
  0.0 53.8 %shard_map.28 = f32[3,8,8,128]{3,2,1,0:T(8,128)} custom-call(f32[3,8,8,128]{3,2,1,0:T(8,128)} %loads.1, f32[8,8,128]{2,1,0:T(8,128)} %density.1), custom_call_target="tpu_custom_call" | custom-call | flops 100000000 | bytes 1000000 | tf_op jit(solution)/shard_map/pallas_call | solution.py:712
  53.8 1.5 %copy.4 = f32[3,8,8,128]{3,2,1,0:T(8,128)} copy(f32[3,8,8,128]{3,2,1,0:T(8,128)} %shard_map.28) | data formatting | bytes 196608

commit v6 on v5

--- a/solution.py
+++ b/solution.py
@@ -14,9 +14,9 @@
 SIDE = 8
 UNROLL = 16
 ZHALO = 12
-RING = (1, 2, 3, 4, -3, -2, -1)
+RING = (4, 3, -3, 2, -2, 1, -1)
 XY8 = [(dx, dy) for dx in (-1, 0, 1) for dy in (-1, 0, 1) if dx or dy]
-YZ23 = [(dy, dz) for dy in (0,) + RING for dz in (-1, 0, 1) if dy or dz]
+YZ23 = [(dy, dz) for dy in RING + (0,) for dz in (-1, 1, 0) if dy or dz]
 
 
 def around():

time: 55.5 us -> 55.1 us (level)
  no operation moved by 1% of the time
where the time goes in v6:
time: 55.1 us; the launch traced here: 55 us
  Pallas kernels  53.4 us (97%)
  local copies, waits for them, and re-layouts  1.54 us (3%)
    pallas_call x1, Pallas kernels, per_device(): pl.pallas_call(kernel, out_shape=jax.ShapeDtypeStruct((3,) + (8,) + TILE,...  53.4 us
    unnamed x1, local copies, waits for them, and re-layouts  1.54 us

profile of v6, /device:TPU:1, one launch (start us, length us, event | category | flops | bytes accessed | tf_op | source)
XLA Modules:
  0.0 55.0 jit_solution(10457615952304326846)
XLA Ops:
  0.0 53.4 %shard_map.28 = f32[3,8,8,128]{3,2,1,0:T(8,128)} custom-call(f32[3,8,8,128]{3,2,1,0:T(8,128)} %loads.1, f32[8,8,128]{2,1,0:T(8,128)} %density.1), custom_call_target="tpu_custom_call" | custom-call | flops 100000000 | bytes 1000000 | tf_op jit(solution)/shard_map/pallas_call | solution.py:712
  53.4 1.5 %copy.4 = f32[3,8,8,128]{3,2,1,0:T(8,128)} copy(f32[3,8,8,128]{3,2,1,0:T(8,128)} %shard_map.28) | data formatting | bytes 196608
